TPU v7x, 512 devices: a whole 4x4x16 slice. The times are simulated.
512 devices in a mesh: section: 32 (over z, core), expert: 16 (over y, x).
Axes of the slice: x: 4, y: 4, z: 16, core: 2. Of those that a mesh axis runs over, the one named last changes fastest.
Arguments:
- held: bfloat16 [32, 3072, 2048], P('section', 'expert'), may hold values from -6 to 6
- entering: bfloat16 [3072, 2048], P('expert'), may hold values from -6 to 6
- norm_gain: bfloat16 [32, 2048], P('section'), may hold values from 0.099609375 to 1.8984375
- router: bfloat16 [32, 2048, 4], P('section'), may hold values from -0.046875 to 0.046875
- w_gate: bfloat16 [32, 2048, 4096], P('section', None, 'expert'), may hold values from -0.125 to 0.125
- w_up: bfloat16 [32, 2048, 4096], P('section', None, 'expert'), may hold values from -0.125 to 0.125
- w_down: bfloat16 [32, 4096, 2048], P('section', 'expert'), may hold values from -0.375 to 0.375
- expert_ids: int32 [32, 3072, 1], P('section', 'expert'), may hold values from 0 to 3; in each aligned block of 192 rows (0 to 191, 192 to 383, ..., all dimensions but the last counted through in order) at most 72 rows name the same one
Outputs:
- mixed: bfloat16 [32, 3072, 2048], P('section', 'expert')
Inputs may be any that keep to these rules, and one draw needn't show every extreme that they name: `expert_ids`: among the 192 tokens of one device at one layer, no expert is chosen more than 72 times, a bound that some block reaches.
All inputs are finite; a program needn't handle non-finite values.
Results may differ from a plain program's by a relative error of at most 0.0055.
Values may be sent and summed in bfloat16 or wider, within the bound.
No kernel may reach another device: no remote copies, remote signals or barrier semaphores. Data moves between devices by JAX's collectives and lax.ppermute only.
A program may use at most 64 MiB of HBM per device.

v0:
```python
import jax
import jax.numpy as jnp
from jax import lax
from jax.sharding import PartitionSpec as P

CAP = 72


def passed_along(block, axis, distance):
    devices = range(lax.axis_size(axis))
    route = [(i - distance, i) for i in devices if i - distance in devices]
    return lax.ppermute(block, axis, route)


def normalize(rows_in, gain_row):
    values = rows_in.astype(jnp.float32)
    scaling = lax.rsqrt(jnp.mean(values * values, axis=-1, keepdims=True) + 1e-06)
    return (values * scaling * gain_row.astype(jnp.float32)).astype(jnp.bfloat16)


def local(held, entering, norm_gain, router, w_gate, w_up, w_down, expert_ids):
    arrived = passed_along(held[0], "section", 1)
    at_first = lax.axis_index("section") == 0
    arriving = jnp.where(at_first, entering, arrived)
    normed = normalize(arriving, norm_gain[0])
    tok_rows = normed.shape[0]
    expert_count = router.shape[2]
    group_size = lax.axis_size("expert")
    panels = group_size // expert_count
    chosen = expert_ids[0, :, 0]
    assigned = chosen[:, None] == jnp.arange(expert_count, dtype=jnp.int32)[None, :]
    positions = jnp.cumsum(assigned.astype(jnp.int32), axis=0) - 1
    position_row = jnp.sum(jnp.where(assigned, positions, 0), axis=1)
    slot_index = jnp.arange(CAP, dtype=jnp.int32)
    selection = assigned.T[:, None, :] & (position_row[None, None, :] == slot_index[None, :, None])
    select_mat = selection.astype(jnp.bfloat16)
    own_expert = lax.axis_index("expert") // panels
    piece_rows = lax.all_gather(normed, "expert", axis=0, tiled=True)
    labels = lax.all_gather(chosen[:, None].astype(jnp.bfloat16), "expert", axis=0, tiled=True)
    sources = piece_rows.shape[0] // tok_rows
    labels = labels.reshape(sources, tok_rows).astype(jnp.int32)
    matches = labels == own_expert
    places = jnp.cumsum(matches.astype(jnp.int32), axis=1) - 1
    picked = matches[:, None, :] & (places[:, None, :] == slot_index[None, :, None])
    placed = jnp.einsum(
        "scr,srd->scd",
        picked.astype(jnp.bfloat16),
        piece_rows.reshape(sources, tok_rows, -1),
        preferred_element_type=jnp.float32,
    ).astype(jnp.bfloat16)
    gate_proj = jnp.einsum("snd,du->snu", placed, w_gate[0], preferred_element_type=jnp.float32)
    up_proj = jnp.einsum("snd,du->snu", placed, w_up[0], preferred_element_type=jnp.float32)
    hidden = (jax.nn.silu(gate_proj) * up_proj).astype(jnp.bfloat16)
    returned = lax.all_to_all(
        jnp.einsum("snu,ud->snd", hidden, w_down[0], preferred_element_type=jnp.float32).astype(
            jnp.bfloat16
        ),
        "expert",
        split_axis=0,
        concat_axis=0,
        tiled=True,
    )
    grouped = returned.reshape(expert_count, panels, CAP, -1)
    mixture = jnp.einsum("ecr,epcd->rd", select_mat, grouped, preferred_element_type=jnp.float32)
    logits = jnp.dot(normed, router[0], preferred_element_type=jnp.float32)
    weights = jnp.exp(logits)
    probability = weights / jnp.sum(weights, axis=1, keepdims=True)
    gate_value = jnp.sum(jnp.where(assigned, probability, 0.0), axis=1)
    mixed = (arriving.astype(jnp.float32) + gate_value[:, None] * mixture).astype(jnp.bfloat16)
    return mixed[None]


def solution(mesh):
    placed = (
        P("section", "expert", None),
        P("expert", None),
        P("section", None),
        P("section", None, None),
        P("section", None, "expert"),
        P("section", None, "expert"),
        P("section", "expert", None),
        P("section", "expert", None),
    )
    return jax.shard_map(
        local, mesh=mesh, in_specs=placed, out_specs=P("section", "expert", None), check_vma=False
    )
```

profile of v0, /device:TPU:1, one launch (start us, length us, event | category | flops | bytes accessed | tf_op | source)
XLA Modules:
  0.0 241.7 jit_solution(6087309761525091625)
XLA Ops:
  6.5 0.0 copy-start
  6.5 0.0 all-gather.3.cloned.1.call-start
  6.5 5.1 %collective-permute-start = (bf16[192,2048]{1,0:T(8,128)(2,1)}, bf16[192,2048]{1,0:T(8,128)(2,1)S(1)}, u32[]{:S(2)}, u32[]{:S(2)}) collective-permute-start(bf16[192,2048]{1,0:T(8,128)(2,1)} %bitcast.69), channel_id=1, source_target_pairs={{0,16},{16,32},{32,48},{48,64},{64,80},{80,96},{96,112},{112,128},... | collective-permute-start | bytes 2359304 | tf_op jit(solution)/shard_map/ppermute | solution.py:12
  11.6 0.7 mul.50
  12.3 8.5 %collective-permute-done = bf16[192,2048]{1,0:T(8,128)(2,1)S(1)} collective-permute-done((bf16[192,2048]{1,0:T(8,128)(2,1)}, bf16[192,2048]{1,0:T(8,128)(2,1)S(1)}, u32[]{:S(2)}, u32[]{:S(2)}) %collective-permute-start) | collective-permute-done | bytes 786464 | tf_op jit(solution)/shard_map/ppermute | solution.py:12
  20.8 0.4 fusion.4
  21.2 1.1 fusion.6
  22.3 0.0 all-gather.3.cloned.1.call-update
  22.4 1.3 dynamic-slice
  24.3 0.0 copy-done.4
  24.3 0.2 dynamic-update-slice
  24.6 34.3 %all-reduce.2 = bf16[3072]{0:T(1024)(128)(2,1)S(1)} all-reduce(bf16[3072]{0:T(1024)(128)(2,1)S(1)} %dynamic-update-slice), channel_id=2, replica_groups=mesh['section'=32,'expert'=16] {'expert'}, use_global_device_ids=true, to_apply=%add.2 | all-reduce | flops 3072 | bytes 12288
  58.9 0.1 eq.87
  59.0 0.6 reduce-window.16
  59.6 0.2 slice_reduce_fusion
  59.8 0.1 copy_bitcast_fusion
  59.9 73.8 %all-gather.3.cloned.1.call-done = bf16[3072,2048]{1,0:T(8,128)(2,1)} async-done(((bf16[192,2048]{1,0:T(8,128)(2,1)}), bf16[3072,2048]{1,0:T(8,128)(2,1)}) %all-gather.3.cloned.1.call-update) | async-done | bytes 12582928 | tf_op jit(solution)/shard_map/all_gather | solution.py:38
  133.7 6.9 %convolution_convert_fusion = bf16[16,72,2048]{2,1,0:T(8,128)(2,1)S(1)} fusion(bf16[16,192,2048]{2,1,0:T(8,128)(2,1)} %bitcast.62, s32[16,192]{1,0:T(8,128)S(1)} %slice_add_fusion, pred[16,192]{1,0:T(8,128)(4,1)S(1)} %eq.87), kind=kOutput, calls=%fused_computation.1 | convolution fusion | flops 908771328 | bytes 17316864 | tf_op jit(solution)/shard_map/scr,srd->scd/dot_general | solution.py:45
  140.7 2.2 copy-done.1
  142.8 0.0 copy-done.5
  142.8 2.5 %fusion.18 = f32[16,72,256]{2,1,0:T(8,128)} fusion(bf16[16,72,2048]{2,1,0:T(8,128)(2,1)S(1)} %convolution_convert_fusion, bf16[1,2048,256]{2,1,0:T(8,128)(2,1)S(1)} %copy-done.5), kind=kOutput, calls=%fused_computation.25 | convolution fusion | flops 1207959552 | bytes 6946816 | tf_op jit(solution)/shard_map/snd,du->snu/dot_general | solution.py:51
  145.3 9.7 %convolution_convert_fusion.1 = bf16[16,72,2048]{2,1,0:T(8,128)(2,1)} fusion(bf16[16,72,2048]{2,1,0:T(8,128)(2,1)} %copy-done.1, f32[16,72,256]{2,1,0:T(8,128)} %fusion.18, bf16[1,256,2048]{2,1,0:T(8,128)(2,1)S(1)} %copy-done, bf16[1,2048,256]{2,1,0:T(8,128)(2,1)S(1)} %copy-done.6), kind=kOutput, calls=%fused_computation.2 | convolution fusion | flops 2420047872 | bytes 12713984 | tf_op jit(solution)/shard_map/snu,ud->snd/dot_general | solution.py:55
  155.1 5.2 %all-to-all-start = ((bf16[16,72,2048]{2,1,0:T(8,128)(2,1)}), bf16[16,72,2048]{2,1,0:T(8,128)(2,1)}, u32[]{:S(2)}, u32[]{:S(2)}) async-start(bf16[16,72,2048]{2,1,0:T(8,128)(2,1)} %convolution_convert_fusion.1), calls=%async_computation | async-start | bytes 9437184 | tf_op jit(solution)/shard_map/all_to_all | solution.py:54
  160.3 1.2 reduce-window.14
  161.5 0.1 slice.24
  161.6 0.1 copy.11
  161.7 0.1 copy.12
  161.8 0.1 add_bitcast_fusion.1
  162.0 0.3 fusion.31
  162.3 67.7 %all-to-all-done = bf16[16,72,2048]{2,1,0:T(8,128)(2,1)} async-done(((bf16[16,72,2048]{2,1,0:T(8,128)(2,1)}), bf16[16,72,2048]{2,1,0:T(8,128)(2,1)}, u32[]{:S(2)}, u32[]{:S(2)}) %all-to-all-start) | async-done | bytes 4718624 | tf_op jit(solution)/shard_map/all_to_all | solution.py:54
  230.1 3.3 %convert_reduce_fusion = bf16[4,72,2048]{2,1,0:T(8,128)(2,1)S(1)} fusion(bf16[16,72,2048]{2,1,0:T(8,128)(2,1)} %all-to-all-done), kind=kLoop, calls=%fused_computation | loop fusion | flops 4128768 | bytes 5898240 | tf_op jit(solution)/shard_map/ecr,epcd->rd/reduce_sum | solution.py:64
  233.4 1.5 fusion.3
  (27 shorter events, 0.3 us)
Async XLA Ops:
  6.5 138.8 %copy-start = (bf16[1,256,2048]{2,1,0:T(8,128)(2,1)S(1)}, bf16[1,256,2048]{2,1,0:T(8,128)(2,1)}, u32[]{:S(2)}) copy-start(bf16[1,256,2048]{2,1,0:T(8,128)(2,1)} %param.14) | copy-start | bytes 3145732
  6.5 127.2 %all-gather.3.cloned.1.call-start = ((), (), s32[]{:S(2)}) async-start(), calls=%async_computation.1 | async-start | bytes 13369344 | tf_op jit(solution)/shard_map/all_gather | solution.py:38
  6.5 14.3 %collective-permute-start = (bf16[192,2048]{1,0:T(8,128)(2,1)}, bf16[192,2048]{1,0:T(8,128)(2,1)S(1)}, u32[]{:S(2)}, u32[]{:S(2)}) collective-permute-start(bf16[192,2048]{1,0:T(8,128)(2,1)} %bitcast.69), channel_id=1, source_target_pairs={{0,16},{16,32},{32,48},{48,64},{64,80},{80,96},{96,112},{112,128},... | collective-permute-start | bytes 2359304 | tf_op jit(solution)/shard_map/ppermute | solution.py:12
  21.2 3.1 %copy-start.4 = (s32[1,192,1]{1,2,0:T(1,128)S(1)}, s32[1,192,1]{1,2,0:T(1,128)}, u32[]{:S(2)}) copy-start(s32[1,192,1]{1,2,0:T(1,128)} %param.15) | copy-start | bytes 2308
  133.7 9.1 %copy-start.5 = (bf16[1,2048,256]{2,1,0:T(8,128)(2,1)S(1)}, bf16[1,2048,256]{2,1,0:T(8,128)(2,1)}, u32[]{:S(2)}) copy-start(bf16[1,2048,256]{2,1,0:T(8,128)(2,1)} %param.12) | copy-start | bytes 3145732
  140.7 2.2 copy-start.1
  142.8 2.5 %copy-start.6 = (bf16[1,2048,256]{2,1,0:T(8,128)(2,1)S(1)}, bf16[1,2048,256]{2,1,0:T(8,128)(2,1)}, u32[]{:S(2)}) copy-start(bf16[1,2048,256]{2,1,0:T(8,128)(2,1)} %param.13) | copy-start | bytes 3145732
  155.1 6.9 %copy-start.2 = (bf16[192,2048]{1,0:T(8,128)(2,1)S(1)}, bf16[192,2048]{1,0:T(8,128)(2,1)}, u32[]{:S(2)}) copy-start(bf16[192,2048]{1,0:T(8,128)(2,1)} %fusion.6) | copy-start | bytes 2359300
  155.1 6.9 %copy-start.3 = (bf16[1,2048,4]{1,2,0:T(4,128)(2,1)S(1)}, bf16[1,2048,4]{1,2,0:T(4,128)(2,1)}, u32[]{:S(2)}) copy-start(bf16[1,2048,4]{1,2,0:T(4,128)(2,1)} %param.11) | copy-start | bytes 49156
  155.1 75.0 %all-to-all-start = ((bf16[16,72,2048]{2,1,0:T(8,128)(2,1)}), bf16[16,72,2048]{2,1,0:T(8,128)(2,1)}, u32[]{:S(2)}, u32[]{:S(2)}) async-start(bf16[16,72,2048]{2,1,0:T(8,128)(2,1)} %convolution_convert_fusion.1), calls=%async_computation | async-start | bytes 9437184 | tf_op jit(solution)/shard_map/all_to_all | solution.py:54
Sparse Core Ops, SparseCore 0:
  22.5 111.1 all-gather.2
where the time goes:
time: 242 us
  waiting for transfers between devices  150 us (62%)
  blocking collectives  34.3 us (14%)
  matrix products  21 us (9%)
  between operations  14.2 us (6%)
  starting transfers between devices  10.2 us (4%)
  other arithmetic  7.68 us (3%)
  local copies, waits for them, and re-layouts  4.31 us (2%)
    all_gather x1, waiting for transfers between devices, local(): piece_rows = lax.all_gather(normed, 'expert', axis=0, tiled=True)  73.8 us
    all_to_all x1, waiting for transfers between devices, local(): lax.all_to_all(jnp.einsum('snu,ud->snd', hidden, w_down[0], preferred_ele...  67.7 us
    unnamed x1, blocking collectives  34.3 us
    dot_general x1, matrix products, local(): jnp.einsum('snu,ud->snd', hidden, w_down[0], preferred_element_type=jnp.f...  9.71 us
    ppermute x1, waiting for transfers between devices, passed_along(): return lax.ppermute(block, axis, route)  8.51 us
    dot_general x1, matrix products, local(): jnp.einsum('scr,srd->scd', picked.astype(jnp.bfloat16), piece_rows.reshap...  6.94 us
    all_to_all x1, starting transfers between devices, local(): lax.all_to_all(jnp.einsum('snu,ud->snd', hidden, w_down[0], preferred_ele...  5.15 us
    ppermute x1, starting transfers between devices, passed_along(): return lax.ppermute(block, axis, route)  5.05 us
  transfers between devices with their start and end apart: 3, of which 3 were waited for; matrix products, arithmetic and copies ran while one was open for 2% of the time, Pallas kernels for 0%

commit v1 on v0

v1 whole, which is shorter than its diff:
```python
import jax
import jax.numpy as jnp
from jax import lax
from jax.sharding import PartitionSpec as P

CAP = 72


def passed_along(block, axis, distance):
    devices = range(lax.axis_size(axis))
    route = [(i - distance, i) for i in devices if i - distance in devices]
    return lax.ppermute(block, axis, route)


def normalize(rows_in, gain_row):
    values = rows_in.astype(jnp.float32)
    scaling = lax.rsqrt(jnp.mean(values * values, axis=-1, keepdims=True) + 1e-06)
    return (values * scaling * gain_row.astype(jnp.float32)).astype(jnp.bfloat16)


def local(held, entering, norm_gain, router, w_gate, w_up, w_down, expert_ids):
    experts = router.shape[2]
    panels = lax.axis_size("expert") // experts
    along_row = [[e * panels + p for p in range(panels)] for e in range(experts)]
    along_column = [[e * panels + p for e in range(experts)] for p in range(panels)]
    tokens, features = entering.shape
    slots = experts * CAP

    down = lax.all_gather(w_down[0], "expert", axis_index_groups=along_row, axis=0, tiled=True)

    chosen = expert_ids[0, :, 0]
    assigned = chosen[:, None] == jnp.arange(experts, dtype=jnp.int32)[None, :]
    earlier = jnp.tril(jnp.ones((tokens, tokens), jnp.bfloat16), -1)
    ranks = jnp.dot(earlier, assigned.astype(jnp.bfloat16), preferred_element_type=jnp.float32)
    place = jnp.sum(jnp.where(assigned, ranks, 0.0), axis=1).astype(jnp.int32) + chosen * CAP
    slot_index = jnp.arange(slots, dtype=jnp.int32)
    select = (place[None, :] == slot_index[:, None]).astype(jnp.bfloat16)
    spread = (place[:, None] == slot_index[None, :]).astype(jnp.bfloat16)

    arrived = passed_along(held[0], "section", 1)
    arriving = jnp.where(lax.axis_index("section") == 0, entering, arrived)
    normed = normalize(arriving, norm_gain[0])
    sent = jnp.dot(select, normed, preferred_element_type=jnp.float32).astype(jnp.bfloat16)

    mine = lax.all_to_all(
        sent, "expert", split_axis=0, concat_axis=0, axis_index_groups=along_column, tiled=True
    )
    rows = lax.all_gather(mine, "expert", axis_index_groups=along_row, axis=0, tiled=True)

    gate_proj = jnp.dot(rows, w_gate[0], preferred_element_type=jnp.float32)
    up_proj = jnp.dot(rows, w_up[0], preferred_element_type=jnp.float32)
    hidden = (jax.nn.silu(gate_proj) * up_proj).astype(jnp.bfloat16)
    own = lax.all_to_all(
        hidden, "expert", split_axis=0, concat_axis=0, axis_index_groups=along_row, tiled=True
    )
    units = hidden.shape[1]
    own = own.reshape(panels, slots, units)
    wide = own.transpose(1, 0, 2).reshape(slots, panels * units)
    total = jnp.dot(wide, down, preferred_element_type=jnp.float32).astype(jnp.bfloat16)
    returned = lax.all_to_all(
        total, "expert", split_axis=0, concat_axis=0, axis_index_groups=along_column, tiled=True
    )
    mixture = jnp.dot(spread, returned, preferred_element_type=jnp.float32)

    logits = jnp.dot(normed, router[0], preferred_element_type=jnp.float32)
    weights = jnp.exp(logits)
    probability = weights / jnp.sum(weights, axis=1, keepdims=True)
    gate_value = jnp.sum(jnp.where(assigned, probability, 0.0), axis=1)
    mixed = (arriving.astype(jnp.float32) + gate_value[:, None] * mixture).astype(jnp.bfloat16)
    return mixed[None]


def solution(mesh):
    placed = (
        P("section", "expert", None),
        P("expert", None),
        P("section", None),
        P("section", None, None),
        P("section", None, "expert"),
        P("section", None, "expert"),
        P("section", "expert", None),
        P("section", "expert", None),
    )
    return jax.shard_map(
        local, mesh=mesh, in_specs=placed, out_specs=P("section", "expert", None), check_vma=False
    )
```

time: 242 us -> 196 us (0.81)
  waiting for transfers between devices: 150 us -> 128 us
  matrix products: 21 us -> 13.5 us
  other arithmetic: 7.68 us -> 1.82 us
  blocking collectives: 34.3 us -> 29.9 us
  local copies, waits for them, and re-layouts: 4.31 us -> 0.08 us
    all_to_all x1, waiting for transfers between devices: 67.7 us -> 15.1 us  [local(): lax.all_to_all(total, 'expert', split_axis=0, concat_axis=0, axis_index_g...]
    unnamed x1 -> x0, blocking collectives: 34.3 us -> none
    all_gather x1 -> x2, waiting for transfers between devices: 73.8 us -> 105 us  [the longest x1 64.1 us: local(): lax.all_gather(mine, 'expert', axis_index_groups=along_row, axis=0, tiled...]
    all_to_all x0 -> x2, blocking collectives: none -> 29.9 us  [the longest x1 18 us: local(): lax.all_to_all(sent, 'expert', split_axis=0, concat_axis=0, axis_index_gr...]
    dot_general x4 -> x6, matrix products: 20.7 us -> 13.1 us  [the longest x1 4.59 us: local(): jnp.dot(wide, down, preferred_element_type=jnp.float32).astype(jnp.bfloat16)]
    unnamed x18 -> x10, local copies, waits for them, and re-layouts: 3.74 us -> 0.02 us
    reduce_sum x2 -> x0, other arithmetic: 3.33 us -> none  [the longest x1 3.31 us: local(): jnp.einsum('ecr,epcd->rd', select_mat, grouped, preferred_element_type=jn...]
  transfers between devices with their start and end apart: 3 -> 4, of which waited for: 3 -> 4; matrix products, arithmetic and copies ran while one was open for 2% -> 4% of each run, Pallas kernels for 0% -> 0%
where the time goes in v1:
time: 196 us
  waiting for transfers between devices  128 us (65%)
  blocking collectives  29.9 us (15%)
  matrix products  13.5 us (7%)
  between operations  13.5 us (7%)
  starting transfers between devices  9.23 us (5%)
    all_gather x1, waiting for transfers between devices, local(): lax.all_gather(mine, 'expert', axis_index_groups=along_row, axis=0, tiled...  64.1 us
    all_gather x1, waiting for transfers between devices, local(): lax.all_gather(w_down[0], 'expert', axis_index_groups=along_row, axis=0,...  41.1 us
    all_to_all x1, blocking collectives, local(): lax.all_to_all(sent, 'expert', split_axis=0, concat_axis=0, axis_index_gr...  18 us
    all_to_all x1, waiting for transfers between devices, local(): lax.all_to_all(total, 'expert', split_axis=0, concat_axis=0, axis_index_g...  15.1 us
    all_to_all x1, blocking collectives, local(): lax.all_to_all(hidden, 'expert', split_axis=0, concat_axis=0, axis_index_...  11.9 us
    ppermute x1, waiting for transfers between devices, passed_along(): return lax.ppermute(block, axis, route)  6.81 us
    ppermute x1, starting transfers between devices, passed_along(): return lax.ppermute(block, axis, route)  5.05 us
    dot_general x1, matrix products, local(): jnp.dot(wide, down, preferred_element_type=jnp.float32).astype(jnp.bfloat16)  4.59 us
  transfers between devices with their start and end apart: 4, of which 4 were waited for; matrix products, arithmetic and copies ran while one was open for 4% of the time, Pallas kernels for 0%

profile of v1, /device:TPU:1, one launch (start us, length us, event | category | flops | bytes accessed | tf_op | source)
XLA Modules:
  0.0 195.9 jit_solution(15174047873946157349)
XLA Ops:
  6.5 0.0 copy-start
  6.5 0.0 all-gather.4.cloned.1.call-start
  6.5 5.1 %collective-permute-start = (bf16[192,2048]{1,0:T(8,128)(2,1)}, bf16[192,2048]{1,0:T(8,128)(2,1)S(1)}, u32[]{:S(2)}, u32[]{:S(2)}) collective-permute-start(bf16[192,2048]{1,0:T(8,128)(2,1)} %bitcast.45), channel_id=1, source_target_pairs={{0,16},{16,32},{32,48},{48,64},{64,80},{80,96},{96,112},{112,128},... | collective-permute-start | bytes 2359304 | tf_op jit(solution)/shard_map/ppermute | solution.py:12
  11.6 0.7 mul.66
  12.3 1.0 fusion.12
  13.3 0.7 multiply_add_fusion
  14.0 6.8 %collective-permute-done = bf16[192,2048]{1,0:T(8,128)(2,1)S(1)} collective-permute-done((bf16[192,2048]{1,0:T(8,128)(2,1)}, bf16[192,2048]{1,0:T(8,128)(2,1)S(1)}, u32[]{:S(2)}, u32[]{:S(2)}) %collective-permute-start) | collective-permute-done | bytes 786464 | tf_op jit(solution)/shard_map/ppermute | solution.py:12
  20.8 0.4 fusion.9
  21.2 0.6 convolution_convert_fusion
  21.8 18.0 %all_to_all.33 = bf16[4,72,2048]{2,1,0:T(8,128)(2,1)} all-to-all(bf16[4,72,2048]{2,1,0:T(8,128)(2,1)S(1)} %bitcast.37), channel_id=1, replica_groups={{0,4,8,12},{1,5,9,13},{2,6,10,14},{3,7,11,15},{16,20,24,28},{17,21,25,2..., dimensions={0} | all-to-all | bytes 2359296 | tf_op jit(solution)/shard_map/all_to_all | solution.py:45
  39.8 0.0 all-gather.4.cloned.1.call-update
  39.9 0.0 all-gather.6.cloned.1.call-start
  39.9 0.7 all-gather.6.cloned.1.call-update
  40.6 0.0 copy-start.3
  40.6 64.1 %all-gather.4.cloned.1.call-done = bf16[1152,2048]{1,0:T(8,128)(2,1)} async-done(((bf16[288,2048]{1,0:T(8,128)(2,1)}), bf16[1152,2048]{1,0:T(8,128)(2,1)}) %all-gather.4.cloned.1.call-update) | async-done | bytes 4718608 | tf_op jit(solution)/shard_map/all_gather | solution.py:48
  104.7 0.0 copy-done
  104.7 0.0 copy-start.2
  104.7 3.9 %fusion.14 = f32[1152,256]{1,0:T(8,128)S(1)} fusion(bf16[1152,2048]{1,0:T(8,128)(2,1)} %all-gather.4.cloned.1.call-done, bf16[1,2048,256]{2,1,0:T(8,128)(2,1)S(1)} %copy-done), kind=kOutput, calls=%fused_computation.19 | convolution fusion | flops 1207959552 | bytes 6946816 | tf_op jit(solution)/shard_map/dot_general | solution.py:50
  108.6 0.0 copy-done.3
  108.6 0.0 copy-done.2
  108.6 1.6 fusion.5
  110.2 11.9 %all_to_all.34 = bf16[4,288,256]{2,1,0:T(8,128)(2,1)S(1)} all-to-all(bf16[4,288,256]{2,1,0:T(8,128)(2,1)S(1)} %bitcast.39), channel_id=1, replica_groups={{0,1,2,3},{4,5,6,7},{8,9,10,11},{12,13,14,15},{16,17,18,19},{20,21,22,2..., dimensions={0} | all-to-all | bytes 1179648 | tf_op jit(solution)/shard_map/all_to_all | solution.py:53
  122.1 0.1 copy.11
  122.2 41.1 %all-gather.6.cloned.1.call-done = bf16[1,1024,2048]{2,1,0:T(8,128)(2,1)} async-done(((bf16[1,256,2048]{2,1,0:T(8,128)(2,1)}), bf16[1,1024,2048]{2,1,0:T(8,128)(2,1)}) %all-gather.6.cloned.1.call-update) | async-done | bytes 4194320 | tf_op jit(solution)/shard_map/all_gather | solution.py:29
  163.2 4.6 %fusion.2 = bf16[288,2048]{1,0:T(8,128)(2,1)} fusion(bf16[288,1024]{1,0:T(8,128)(2,1)S(1)} %bitcast.38, bf16[1,1024,2048]{2,1,0:T(8,128)(2,1)} %all-gather.6.cloned.1.call-done), kind=kOutput, calls=%fused_computation.4 | convolution fusion | flops 1208549376 | bytes 5963776 | tf_op jit(solution)/shard_map/dot_general | solution.py:59
  167.8 0.0 copy-start.4
  167.8 4.1 %all-to-all-start.2 = ((bf16[4,72,2048]{2,1,0:T(8,128)(2,1)}), bf16[4,72,2048]{2,1,0:T(8,128)(2,1)S(1)}, u32[]{:S(2)}, u32[]{:S(2)}) async-start(bf16[4,72,2048]{2,1,0:T(8,128)(2,1)} %bitcast.36), calls=%async_computation.2 | async-start | bytes 2359296 | tf_op jit(solution)/shard_map/all_to_all | solution.py:60
  172.0 0.0 copy-done.4
  172.0 0.4 fusion.30
  172.4 0.0 copy-done.1
  172.4 15.1 %all-to-all-done.2 = bf16[4,72,2048]{2,1,0:T(8,128)(2,1)S(1)} async-done(((bf16[4,72,2048]{2,1,0:T(8,128)(2,1)}), bf16[4,72,2048]{2,1,0:T(8,128)(2,1)S(1)}, u32[]{:S(2)}, u32[]{:S(2)}) %all-to-all-start.2) | async-done | bytes 1179680 | tf_op jit(solution)/shard_map/all_to_all | solution.py:60
  187.6 1.5 fusion.8
  (4 shorter events, 0.0 us)
Async XLA Ops:
  6.5 98.2 %copy-start = (bf16[1,2048,256]{2,1,0:T(8,128)(2,1)S(1)}, bf16[1,2048,256]{2,1,0:T(8,128)(2,1)}, u32[]{:S(2)}) copy-start(bf16[1,2048,256]{2,1,0:T(8,128)(2,1)} %param.12) | copy-start | bytes 3145732
  6.5 98.2 %all-gather.4.cloned.1.call-start = ((), (), s32[]{:S(2)}) async-start(), calls=%async_computation.3 | async-start | bytes 5898240 | tf_op jit(solution)/shard_map/all_gather | solution.py:48
  6.5 14.3 %collective-permute-start = (bf16[192,2048]{1,0:T(8,128)(2,1)}, bf16[192,2048]{1,0:T(8,128)(2,1)S(1)}, u32[]{:S(2)}, u32[]{:S(2)}) collective-permute-start(bf16[192,2048]{1,0:T(8,128)(2,1)} %bitcast.45), channel_id=1, source_target_pairs={{0,16},{16,32},{32,48},{48,64},{64,80},{80,96},{96,112},{112,128},... | collective-permute-start | bytes 2359304 | tf_op jit(solution)/shard_map/ppermute | solution.py:12
  39.9 123.4 %all-gather.6.cloned.1.call-start = ((), (), s32[]{:S(2)}) async-start(), calls=%async_computation.4 | async-start | bytes 5242880 | tf_op jit(solution)/shard_map/all_gather | solution.py:29
  40.6 68.0 %copy-start.3 = (bf16[1,2048,256]{2,1,0:T(8,128)(2,1)S(1)}, bf16[1,2048,256]{2,1,0:T(8,128)(2,1)}, u32[]{:S(2)}) copy-start(bf16[1,2048,256]{2,1,0:T(8,128)(2,1)} %param.13) | copy-start | bytes 3145732
  104.7 3.9 %copy-start.2 = (bf16[1152,2048]{1,0:T(8,128)(2,1)S(1)}, bf16[1152,2048]{1,0:T(8,128)(2,1)}, u32[]{:S(2)}) copy-start(bf16[1152,2048]{1,0:T(8,128)(2,1)} %all-gather.4.cloned.1.call-done) | copy-start | bytes 14155780
  167.8 4.1 %copy-start.4 = (bf16[1,2048,4]{1,2,0:T(4,128)(2,1)S(1)}, bf16[1,2048,4]{1,2,0:T(4,128)(2,1)}, u32[]{:S(2)}) copy-start(bf16[1,2048,4]{1,2,0:T(4,128)(2,1)} %param.11) | copy-start | bytes 49156
  167.8 4.5 %copy-start.1 = (s32[1,192,1]{1,2,0:T(1,128)S(1)}, s32[1,192,1]{1,2,0:T(1,128)}, u32[]{:S(2)}) copy-start(s32[1,192,1]{1,2,0:T(1,128)} %param.15) | copy-start | bytes 2308
  167.8 19.7 %all-to-all-start.2 = ((bf16[4,72,2048]{2,1,0:T(8,128)(2,1)}), bf16[4,72,2048]{2,1,0:T(8,128)(2,1)S(1)}, u32[]{:S(2)}, u32[]{:S(2)}) async-start(bf16[4,72,2048]{2,1,0:T(8,128)(2,1)} %bitcast.36), calls=%async_computation.2 | async-start | bytes 2359296 | tf_op jit(solution)/shard_map/all_to_all | solution.py:60
Sparse Core Ops, SparseCore 0:
  40.0 64.6 all-gather.3
  106.8 56.4 all-gather.5

commit v2 on v1

v2 whole, which is shorter than its diff:
```python
import jax
import jax.numpy as jnp
from jax import lax
from jax.experimental import pallas as pl
from jax.experimental.pallas import tpu as pltpu
from jax.sharding import PartitionSpec as P

CAP = 72
VMEM_BYTES = 40 * 1024 * 1024


def passed_along(block, axis, distance):
    devices = range(lax.axis_size(axis))
    route = [(i - distance, i) for i in devices if i - distance in devices]
    return lax.ppermute(block, axis, route)


def normalize(rows_in, gain_row):
    values = rows_in.astype(jnp.float32)
    scaling = lax.rsqrt(jnp.mean(values * values, axis=-1, keepdims=True) + 1e-06)
    return (values * scaling * gain_row.astype(jnp.float32)).astype(jnp.bfloat16)


def product(left, right):
    return jnp.dot(left, right, preferred_element_type=jnp.float32)


def whole(shape):
    return pl.BlockSpec(shape, lambda i: (0, 0))


def hidden_kernel(rows_ref, gate_ref, up_ref, hidden_ref):
    rows = rows_ref[...]
    gate_proj = product(rows, gate_ref[...])
    up_proj = product(rows, up_ref[...])
    hidden_ref[...] = (jax.nn.silu(gate_proj) * up_proj).astype(hidden_ref.dtype)


def hidden_units(rows, gate, up, steps=4):
    count, features = rows.shape
    units = gate.shape[1]
    block = count // steps
    return pl.pallas_call(
        hidden_kernel,
        grid=(steps,),
        out_shape=jax.ShapeDtypeStruct((count, units), jnp.bfloat16),
        in_specs=[
            pl.BlockSpec((block, features), lambda i: (i, 0)),
            whole((features, units)),
            whole((features, units)),
        ],
        out_specs=pl.BlockSpec((block, units), lambda i: (i, 0)),
        compiler_params=pltpu.CompilerParams(vmem_limit_bytes=VMEM_BYTES),
        cost_estimate=pl.CostEstimate(
            flops=4 * count * features * units,
            bytes_accessed=2 * (count * (features + units) + 2 * features * units),
            transcendentals=count * units,
        ),
    )(rows, gate, up)


def down_kernel(hidden_ref, other_ref, down_ref, down_other_ref, part_ref):
    total = product(hidden_ref[...], down_ref[...])
    total += product(other_ref[...], down_other_ref[...])
    part_ref[...] = total.astype(part_ref.dtype)


def down_part(hidden, other, down, down_other, steps=4):
    count, units = hidden.shape
    features = down.shape[1]
    block = features // steps
    return pl.pallas_call(
        down_kernel,
        grid=(steps,),
        out_shape=jax.ShapeDtypeStruct((count, features), jnp.bfloat16),
        in_specs=[
            whole((count, units)),
            whole((count, units)),
            pl.BlockSpec((units, block), lambda i: (0, i)),
            pl.BlockSpec((units, block), lambda i: (0, i)),
        ],
        out_specs=pl.BlockSpec((count, block), lambda i: (0, i)),
        compiler_params=pltpu.CompilerParams(vmem_limit_bytes=VMEM_BYTES),
        cost_estimate=pl.CostEstimate(
            flops=4 * count * features * units,
            bytes_accessed=2 * (count * (features + 2 * units) + 2 * features * units),
            transcendentals=0,
        ),
    )(hidden, other, down, down_other)


def local(held, entering, norm_gain, router, w_gate, w_up, w_down, expert_ids):
    experts = router.shape[2]
    group = lax.axis_size("expert")
    panels = group // experts
    tokens, features = entering.shape
    swap = [(i, i ^ 1) for i in range(group)]
    column_pairs = [(x, panels - 1 - x) for x in range(panels // 2)]
    token_groups = [[e * panels + x for e in range(experts) for x in pair] for pair in column_pairs]
    copies = 2
    span = copies * CAP
    slots = experts * span

    gate_other = lax.ppermute(w_gate[0], "expert", swap)
    up_other = lax.ppermute(w_up[0], "expert", swap)
    down_other = lax.ppermute(w_down[0], "expert", swap)
    arrived = passed_along(held[0], "section", 1)

    chosen = expert_ids[0, :, 0]
    assigned = chosen[:, None] == jnp.arange(experts, dtype=jnp.int32)[None, :]
    earlier = jnp.tril(jnp.ones((tokens, tokens), jnp.bfloat16), -1)
    ranks = product(earlier, assigned.astype(jnp.bfloat16))
    place = jnp.sum(jnp.where(assigned, ranks, 0.0), axis=1).astype(jnp.int32) + chosen * span
    slot_index = jnp.arange(slots, dtype=jnp.int32)
    row_slot = slot_index - jnp.where(slot_index % span < CAP, 0, CAP)
    select = (place[None, :] == row_slot[:, None]).astype(jnp.bfloat16)
    spread = (place[:, None] == row_slot[None, :]).astype(jnp.bfloat16)

    def dispatch(select, arriving):
        normed = normalize(arriving, norm_gain[0])
        sent = product(select, normed).astype(jnp.bfloat16)
        rows = lax.all_to_all(
            sent, "expert", split_axis=0, concat_axis=0, axis_index_groups=token_groups, tiled=True
        )
        return normed, rows

    def nothing(select, arriving):
        return arriving, jnp.zeros((slots, features), jnp.bfloat16)

    here = lax.axis_index("section") < lax.axis_size("section")
    arriving = jnp.where(lax.axis_index("section") == 0, entering, arrived)
    normed, rows = lax.cond(here, dispatch, nothing, select, arriving)

    hidden = hidden_units(rows, w_gate[0], w_up[0])
    hidden_other = hidden_units(rows, gate_other, up_other)
    part = down_part(hidden, hidden_other, w_down[0], down_other)
    returned = lax.all_to_all(
        part, "expert", split_axis=0, concat_axis=0, axis_index_groups=token_groups, tiled=True
    )
    mixture = product(spread, returned)

    logits = product(normed, router[0])
    weights = jnp.exp(logits)
    probability = weights / jnp.sum(weights, axis=1, keepdims=True)
    gate_value = jnp.sum(jnp.where(assigned, probability, 0.0), axis=1)
    mixed = (arriving.astype(jnp.float32) + gate_value[:, None] * mixture).astype(jnp.bfloat16)
    return mixed[None]


def solution(mesh):
    placed = (
        P("section", "expert", None),
        P("expert", None),
        P("section", None),
        P("section", None, None),
        P("section", None, "expert"),
        P("section", None, "expert"),
        P("section", "expert", None),
        P("section", "expert", None),
    )
    return jax.shard_map(
        local, mesh=mesh, in_specs=placed, out_specs=P("section", "expert", None), check_vma=False
    )
```

time: 196 us -> 121 us (0.62)
  waiting for transfers between devices: 128 us -> 37.4 us
  between operations: 13.5 us -> 0.13 us
  starting transfers between devices: 9.23 us -> 21.7 us
  Pallas kernels: 0 us -> 10.8 us
  matrix products: 13.5 us -> 7.19 us
  blocking collectives: 29.9 us -> 35.5 us
  other arithmetic: 1.82 us -> 5.68 us
    all_gather x2 -> x0, waiting for transfers between devices: 105 us -> none  [the longest x1 64.1 us: local(): lax.all_gather(mine, 'expert', axis_index_groups=along_row, axis=0, tiled...]
    all_to_all x1, waiting for transfers between devices: 15.1 us -> 29.8 us  [local(): lax.all_to_all(part, 'expert', split_axis=0, concat_axis=0, axis_index_gr...]
    pallas_call x0 -> x3, Pallas kernels: none -> 10.8 us  [the longest x2 7.45 us: hidden_units(): pl.pallas_call(hidden_kernel, grid=(steps,), out_shape=jax.ShapeDtypeStru...]
    ppermute x0 -> x3, starting transfers between devices: none -> 8.41 us  [the longest x1 3.12 us: local(): gate_other = lax.ppermute(w_gate[0], 'expert', swap)]
    ppermute x0 -> x3, waiting for transfers between devices: none -> 7.54 us  [the longest x1 7.53 us: local(): down_other = lax.ppermute(w_down[0], 'expert', swap)]
    ppermute x1, waiting for transfers between devices: 6.81 us -> 0.01 us  [passed_along(): return lax.ppermute(block, axis, route)]
    dot_general x7 -> x4, matrix products: 13.5 us -> 7.19 us  [product(): return jnp.dot(left, right, preferred_element_type=jnp.float32)]
    all_to_all x2 -> x1, blocking collectives: 29.9 us -> 35.5 us  [dispatch(): lax.all_to_all(sent, 'expert', split_axis=0, concat_axis=0, axis_index_gr...]
  transfers between devices with their start and end apart: 4 -> 5, of which waited for: 4 -> 2; matrix products, arithmetic and copies ran while one was open for 4% -> 8% of each run, Pallas kernels for 0% -> 6%
where the time goes in v2:
time: 121 us; the launch traced here: 120 us
  waiting for transfers between devices  37.4 us (31%)
  blocking collectives  35.5 us (29%)
  starting transfers between devices  21.7 us (18%)
  Pallas kernels  10.8 us (9%)
  matrix products  7.19 us (6%)
  other arithmetic  5.68 us (5%)
  local copies, waits for them, and re-layouts  1.44 us (1%)
    all_to_all x1, blocking collectives, dispatch(): lax.all_to_all(sent, 'expert', split_axis=0, concat_axis=0, axis_index_gr...  35.5 us
    all_to_all x1, waiting for transfers between devices, local(): lax.all_to_all(part, 'expert', split_axis=0, concat_axis=0, axis_index_gr...  29.8 us
    all_to_all x1, starting transfers between devices, local(): lax.all_to_all(part, 'expert', split_axis=0, concat_axis=0, axis_index_gr...  8.26 us
    ppermute x1, waiting for transfers between devices, local(): down_other = lax.ppermute(w_down[0], 'expert', swap)  7.53 us
    pallas_call x2, Pallas kernels, hidden_units(): pl.pallas_call(hidden_kernel, grid=(steps,), out_shape=jax.ShapeDtypeStru...  7.45 us
    dot_general x4, matrix products, product(): return jnp.dot(left, right, preferred_element_type=jnp.float32)  7.19 us
    ppermute x1, starting transfers between devices, passed_along(): return lax.ppermute(block, axis, route)  5.05 us
    pallas_call x1, Pallas kernels, down_part(): pl.pallas_call(down_kernel, grid=(steps,), out_shape=jax.ShapeDtypeStruct...  3.34 us
  transfers between devices with their start and end apart: 5, of which 2 were waited for; matrix products, arithmetic and copies ran while one was open for 8% of the time, Pallas kernels for 6%

profile of v2, /device:TPU:1, one launch (start us, length us, event | category | flops | bytes accessed | tf_op | source)
XLA Modules:
  0.0 119.9 jit_solution(17326431890955294871)
XLA Ops:
  0.0 0.0 copy-start
  0.0 5.1 %collective-permute-start = (bf16[192,2048]{1,0:T(8,128)(2,1)}, bf16[192,2048]{1,0:T(8,128)(2,1)S(1)}, u32[]{:S(2)}, u32[]{:S(2)}) collective-permute-start(bf16[192,2048]{1,0:T(8,128)(2,1)} %bitcast.36), channel_id=1, source_target_pairs={{0,16},{16,32},{32,48},{48,64},{64,80},{80,96},{96,112},{112,128},... | collective-permute-start | bytes 2359304 | tf_op jit(solution)/shard_map/ppermute | solution.py:15
  5.1 3.1 %collective-permute-start.1 = (bf16[2048,256]{1,0:T(8,128)(2,1)}, bf16[2048,256]{1,0:T(8,128)(2,1)}, u32[]{:S(2)}, u32[]{:S(2)}) collective-permute-start(bf16[2048,256]{1,0:T(8,128)(2,1)} %bitcast.25), channel_id=1, source_target_pairs={{0,1},{1,0},{2,3},{3,2},{4,5},{5,4},{6,7},{7,6},{8,9},{9,8},{10,11... | collective-permute-start | bytes 3145736 | tf_op jit(solution)/shard_map/ppermute | solution.py:104
  8.2 2.2 %collective-permute-start.2 = (bf16[2048,256]{1,0:T(8,128)(2,1)}, bf16[2048,256]{1,0:T(8,128)(2,1)}, u32[]{:S(2)}, u32[]{:S(2)}) collective-permute-start(bf16[2048,256]{1,0:T(8,128)(2,1)} %bitcast.27), channel_id=1, source_target_pairs={{0,1},{1,0},{2,3},{3,2},{4,5},{5,4},{6,7},{7,6},{8,9},{9,8},{10,11... | collective-permute-start | bytes 3145736 | tf_op jit(solution)/shard_map/ppermute | solution.py:105
  10.4 3.1 %collective-permute-start.3 = (bf16[256,2048]{1,0:T(8,128)(2,1)}, bf16[256,2048]{1,0:T(8,128)(2,1)S(1)}, u32[]{:S(2)}, u32[]{:S(2)}) collective-permute-start(bf16[256,2048]{1,0:T(8,128)(2,1)} %bitcast.23), channel_id=1, source_target_pairs={{0,1},{1,0},{2,3},{3,2},{4,5},{5,4},{6,7},{7,6},{8,9},{9,8},{10,11... | collective-permute-start | bytes 3145736 | tf_op jit(solution)/shard_map/ppermute | solution.py:106
  13.5 1.0 fusion.3
  14.5 0.7 multiply_add_fusion
  15.2 0.1 compare_convert_fusion
  15.4 0.0 collective-permute-done
  15.4 1.0 broadcast_select_fusion
  16.4 0.0 copy-done.6
  16.4 41.3 %conditional.1 = (bf16[192,2048]{1,0:T(8,128)(2,1)}, bf16[576,2048]{1,0:T(8,128)(2,1)S(1)}) conditional(s32[]{:T(128)} %convert_element_type.40, bf16[192,2048]{1,0:T(8,128)(2,1)} %broadcast_select_fusion, (bf16[192,2048]{1,0:T(8,128)(2,1)}, bf16[1,2048]{1,0:T(2,128)(2,1)S(1)}, bf16[576,192]{1,0:T(8,128)(2,1)S(1)}) %tuple.17), branch_computations={%region_1.2_spmd, %region_2.4_spmd} | conditional | flops 456919232 | bytes 10468368 | solution.py:132
  16.4 1.5 %fusion = f32[192]{0:T(256)S(1)} fusion(bf16[192,2048]{1,0:T(8,128)(2,1)} %get-tuple-element.12), kind=kLoop, calls=%fused_computation.3 | loop fusion | flops 1179456 | bytes 787200 | tf_op jit(solution)/shard_map/cond/branch_1_fun/reduce_sum | solution.py:20
  17.9 2.3 %fusion.2 = bf16[192,2048]{1,0:T(8,128)(2,1)} fusion(bf16[192,2048]{1,0:T(8,128)(2,1)} %get-tuple-element.12, f32[2048]{0:T(1024)S(1)} %bitcast.32, f32[192]{0:T(256)S(1)} %add_rsqrt_fusion), kind=kLoop, calls=%fused_computation.5 | loop fusion | flops 1572864 | bytes 1581824 | tf_op jit(solution)/shard_map/cond/branch_1_fun/convert_element_type | solution.py:21
  20.2 1.9 %convolution_convert_fusion = bf16[2048,576]{0,1:T(8,128)(2,1)S(1)} fusion(bf16[576,192]{1,0:T(8,128)(2,1)S(1)} %get-tuple-element.14, bf16[192,2048]{1,0:T(8,128)(2,1)} %fusion.2), kind=kOutput, calls=%fused_computation | convolution fusion | flops 454164480 | bytes 3366912 | tf_op jit(solution)/shard_map/cond/branch_1_fun/dot_general | solution.py:25
  22.1 35.5 %all_to_all.21 = bf16[8,72,2048]{2,1,0:T(8,128)(2,1)S(1)} all-to-all(bf16[8,72,2048]{2,1,0:T(8,128)(2,1)S(1)} %bitcast.31), channel_id=1, replica_groups={{0,3,4,7,8,11,12,15},{1,2,5,6,9,10,13,14},{16,19,20,23,24,27,28,31},{17..., dimensions={0} | all-to-all | bytes 4718592 | tf_op jit(solution)/shard_map/cond/branch_1_fun/all_to_all | solution.py:122
  57.6 1.4 %copy-done.4 = bf16[576,2048]{1,0:T(8,128)(2,1)} copy-done((bf16[576,2048]{1,0:T(8,128)(2,1)}, bf16[576,2048]{1,0:T(8,128)(2,1)S(1)}, u32[]{:S(2)}) %copy-start.4) | copy-done | bytes 2359320
  59.0 0.0 copy-done.2
  59.0 0.0 copy-done.3
  59.0 3.8 %shard_map.83.hidden_ref = bf16[576,256]{1,0:T(8,128)(2,1)S(1)} custom-call(bf16[576,2048]{1,0:T(8,128)(2,1)} %copy-done.4, bf16[2048,256]{1,0:T(8,128)(2,1)S(1)} %bitcast.26, bf16[2048,256]{1,0:T(8,128)(2,1)S(1)} %bitcast.28), custom_call_target="tpu_custom_call" | custom-call | flops 1207959552 | bytes 4751360 | tf_op jit(solution)/shard_map/pallas_call | solution.py:43
  62.9 0.0 copy-start.1
  62.9 0.0 collective-permute-done.1.gate_ref
  62.9 0.0 collective-permute-done.2.up_ref
  62.9 0.0 copy-done.5
  62.9 3.6 %shard_map.84.other_ref = bf16[576,256]{1,0:T(8,128)(2,1)S(1)} custom-call(bf16[576,2048]{1,0:T(8,128)(2,1)S(1)} %copy-done.5, bf16[2048,256]{1,0:T(8,128)(2,1)} %collective-permute-done.1.gate_ref, bf16[2048,256]{1,0:T(8,128)(2,1)} %collective-permute-done.2.up_ref), custom_call_target="tpu_custom_call" | custom-call | flops 1207959552 | bytes 4751360 | tf_op jit(solution)/shard_map/pallas_call | solution.py:43
  66.5 7.5 %collective-permute-done.3.down_other_ref = bf16[256,2048]{1,0:T(8,128)(2,1)S(1)} collective-permute-done((bf16[256,2048]{1,0:T(8,128)(2,1)}, bf16[256,2048]{1,0:T(8,128)(2,1)S(1)}, u32[]{:S(2)}, u32[]{:S(2)}) %collective-permute-start.3) | collective-permute-done | bytes 1048608 | tf_op jit(solution)/shard_map/ppermute | solution.py:106
  74.1 3.3 %shard_map.85 = bf16[576,2048]{1,0:T(8,128)(2,1)} custom-call(bf16[576,256]{1,0:T(8,128)(2,1)S(1)} %shard_map.83.hidden_ref, bf16[576,256]{1,0:T(8,128)(2,1)S(1)} %shard_map.84.other_ref, bf16[256,2048]{1,0:T(8,128)(2,1)S(1)} %bitcast.24, bf16[256,2048]{1,0:T(8,128)(2,1)S(1)} %collective-permute-done.3.down_other_ref), custom_call_target="tpu_custom_call" | custom-call | flops 1207959552 | bytes 5046272 | tf_op jit(solution)/shard_map/pallas_call | solution.py:72
  77.4 8.3 %all-to-all-start.1 = ((bf16[8,72,2048]{2,1,0:T(8,128)(2,1)}), bf16[8,72,2048]{2,1,0:T(8,128)(2,1)S(1)}, u32[]{:S(2)}, u32[]{:S(2)}) async-start(bf16[8,72,2048]{2,1,0:T(8,128)(2,1)} %bitcast.10), calls=%async_computation.1 | async-start | bytes 4718592 | tf_op jit(solution)/shard_map/all_to_all | solution.py:137
  85.7 0.0 copy-done
  85.7 1.5 %fusion.22 = (f32[192]{0:T(256)S(1)}, f32[192,4]{0,1:T(4,128)S(1)}) fusion(bf16[192,2048]{1,0:T(8,128)(2,1)} %get-tuple-element.17, bf16[1,2048,4]{1,2,0:T(4,128)(2,1)S(1)} %copy-done), kind=kOutput, calls=%fused_computation.39 | convolution fusion | flops 3146304 | bytes 806656 | tf_op jit(solution)/shard_map/dot_general | solution.py:25
  87.2 29.8 %all-to-all-done.1 = bf16[8,72,2048]{2,1,0:T(8,128)(2,1)S(1)} async-done(((bf16[8,72,2048]{2,1,0:T(8,128)(2,1)}), bf16[8,72,2048]{2,1,0:T(8,128)(2,1)S(1)}, u32[]{:S(2)}, u32[]{:S(2)}) %all-to-all-start.1) | async-done | bytes 2359328 | tf_op jit(solution)/shard_map/all_to_all | solution.py:137
  117.0 2.8 %fusion.4 = bf16[1,192,2048]{2,1,0:T(8,128)(2,1)} fusion(bf16[192,2048]{1,0:T(8,128)(2,1)} %broadcast_select_fusion, bf16[576,2048]{1,0:T(8,128)(2,1)S(1)} %bitcast.30, f32[192]{0:T(256)S(1)} %fusion.17, s32[576]{0:T(1024)S(1)} %iota_subtract_fusion, s32[192]{0:T(256)S(1)} %multiply_add_fusion), kind=kOutput, calls=%fused_computation.12 | convolution fusion | flops 454668288 | bytes 3936000 | tf_op jit(solution)/shard_map/dot_general | solution.py:25
  (13 shorter events, 0.1 us)
Async XLA Ops:
  0.0 85.7 %copy-start = (bf16[1,2048,4]{1,2,0:T(4,128)(2,1)S(1)}, bf16[1,2048,4]{1,2,0:T(4,128)(2,1)}, u32[]{:S(2)}) copy-start(bf16[1,2048,4]{1,2,0:T(4,128)(2,1)} %param.13) | copy-start | bytes 49156
  0.0 16.4 %copy-start.6 = (bf16[1,2048]{1,0:T(2,128)(2,1)S(1)}, bf16[1,2048]{1,0:T(2,128)(2,1)}, u32[]{:S(2)}) copy-start(bf16[1,2048]{1,0:T(2,128)(2,1)} %param.12) | copy-start | bytes 12292
  0.0 15.4 %collective-permute-start = (bf16[192,2048]{1,0:T(8,128)(2,1)}, bf16[192,2048]{1,0:T(8,128)(2,1)S(1)}, u32[]{:S(2)}, u32[]{:S(2)}) collective-permute-start(bf16[192,2048]{1,0:T(8,128)(2,1)} %bitcast.36), channel_id=1, source_target_pairs={{0,16},{16,32},{32,48},{48,64},{64,80},{80,96},{96,112},{112,128},... | collective-permute-start | bytes 2359304 | tf_op jit(solution)/shard_map/ppermute | solution.py:15
  5.1 57.8 %collective-permute-start.1 = (bf16[2048,256]{1,0:T(8,128)(2,1)}, bf16[2048,256]{1,0:T(8,128)(2,1)}, u32[]{:S(2)}, u32[]{:S(2)}) collective-permute-start(bf16[2048,256]{1,0:T(8,128)(2,1)} %bitcast.25), channel_id=1, source_target_pairs={{0,1},{1,0},{2,3},{3,2},{4,5},{5,4},{6,7},{7,6},{8,9},{9,8},{10,11... | collective-permute-start | bytes 3145736 | tf_op jit(solution)/shard_map/ppermute | solution.py:104
  8.2 54.7 %collective-permute-start.2 = (bf16[2048,256]{1,0:T(8,128)(2,1)}, bf16[2048,256]{1,0:T(8,128)(2,1)}, u32[]{:S(2)}, u32[]{:S(2)}) collective-permute-start(bf16[2048,256]{1,0:T(8,128)(2,1)} %bitcast.27), channel_id=1, source_target_pairs={{0,1},{1,0},{2,3},{3,2},{4,5},{5,4},{6,7},{7,6},{8,9},{9,8},{10,11... | collective-permute-start | bytes 3145736 | tf_op jit(solution)/shard_map/ppermute | solution.py:105
  10.4 63.7 %collective-permute-start.3 = (bf16[256,2048]{1,0:T(8,128)(2,1)}, bf16[256,2048]{1,0:T(8,128)(2,1)S(1)}, u32[]{:S(2)}, u32[]{:S(2)}) collective-permute-start(bf16[256,2048]{1,0:T(8,128)(2,1)} %bitcast.23), channel_id=1, source_target_pairs={{0,1},{1,0},{2,3},{3,2},{4,5},{5,4},{6,7},{7,6},{8,9},{9,8},{10,11... | collective-permute-start | bytes 3145736 | tf_op jit(solution)/shard_map/ppermute | solution.py:106
  16.4 42.7 %copy-start.2 = (bf16[1,2048,256]{2,1,0:T(8,128)(2,1)S(1)}, bf16[1,2048,256]{2,1,0:T(8,128)(2,1)}, u32[]{:S(2)}) copy-start(bf16[1,2048,256]{2,1,0:T(8,128)(2,1)} %param.14) | copy-start | bytes 3145732
  16.4 42.7 %copy-start.3 = (bf16[1,2048,256]{2,1,0:T(8,128)(2,1)S(1)}, bf16[1,2048,256]{2,1,0:T(8,128)(2,1)}, u32[]{:S(2)}) copy-start(bf16[1,2048,256]{2,1,0:T(8,128)(2,1)} %param.15) | copy-start | bytes 3145732
  57.6 1.4 %copy-start.4 = (bf16[576,2048]{1,0:T(8,128)(2,1)}, bf16[576,2048]{1,0:T(8,128)(2,1)S(1)}, u32[]{:S(2)}) copy-start(bf16[576,2048]{1,0:T(8,128)(2,1)S(1)} %get-tuple-element.18.rows_ref) | copy-start | bytes 7077892
  59.0 3.9 %copy-start.5 = (bf16[576,2048]{1,0:T(8,128)(2,1)S(1)}, bf16[576,2048]{1,0:T(8,128)(2,1)}, u32[]{:S(2)}) copy-start(bf16[576,2048]{1,0:T(8,128)(2,1)} %copy-done.4) | copy-start | bytes 7077892
  62.9 11.2 %copy-start.1 = (bf16[1,256,2048]{2,1,0:T(8,128)(2,1)S(1)}, bf16[1,256,2048]{2,1,0:T(8,128)(2,1)}, u32[]{:S(2)}) copy-start(bf16[1,256,2048]{2,1,0:T(8,128)(2,1)} %param.16) | copy-start | bytes 3145732
  77.4 9.7 %copy-start.7 = (s32[1,192,1]{1,2,0:T(1,128)S(1)}, s32[1,192,1]{1,2,0:T(1,128)}, u32[]{:S(2)}) copy-start(s32[1,192,1]{1,2,0:T(1,128)} %param.17) | copy-start | bytes 2308
  77.4 39.6 %all-to-all-start.1 = ((bf16[8,72,2048]{2,1,0:T(8,128)(2,1)}), bf16[8,72,2048]{2,1,0:T(8,128)(2,1)S(1)}, u32[]{:S(2)}, u32[]{:S(2)}) async-start(bf16[8,72,2048]{2,1,0:T(8,128)(2,1)} %bitcast.10), calls=%async_computation.1 | async-start | bytes 4718592 | tf_op jit(solution)/shard_map/all_to_all | solution.py:137

commit v3 on v2

--- a/solution.py
+++ b/solution.py
@@ -94,16 +94,26 @@
     group = lax.axis_size("expert")
     panels = group // experts
     tokens, features = entering.shape
-    swap = [(i, i ^ 1) for i in range(group)]
-    column_pairs = [(x, panels - 1 - x) for x in range(panels // 2)]
-    token_groups = [[e * panels + x for e in range(experts) for x in pair] for pair in column_pairs]
+    sections = lax.axis_size("section")
+    everywhere = ("section", "expert")
+    near, mirrored = (lambda x: x ^ 1), (lambda x: panels - 1 - x)
+    swap, token_groups = [], []
+    for section in range(sections):
+        weight_partner, token_partner = (near, mirrored) if section % 2 == 0 else (mirrored, near)
+        start = section * group
+        for i in range(group):
+            swap.append((start + i, start + i - i % panels + weight_partner(i % panels)))
+        for x in range(panels):
+            if x < token_partner(x):
+                pair = (x, token_partner(x))
+                token_groups.append([start + e * panels + c for e in range(experts) for c in pair])
     copies = 2
     span = copies * CAP
     slots = experts * span
 
-    gate_other = lax.ppermute(w_gate[0], "expert", swap)
-    up_other = lax.ppermute(w_up[0], "expert", swap)
-    down_other = lax.ppermute(w_down[0], "expert", swap)
+    gate_other = lax.ppermute(w_gate[0], everywhere, swap)
+    up_other = lax.ppermute(w_up[0], everywhere, swap)
+    down_other = lax.ppermute(w_down[0], everywhere, swap)
     arrived = passed_along(held[0], "section", 1)
 
     chosen = expert_ids[0, :, 0]
@@ -120,7 +130,7 @@
         normed = normalize(arriving, norm_gain[0])
         sent = product(select, normed).astype(jnp.bfloat16)
         rows = lax.all_to_all(
-            sent, "expert", split_axis=0, concat_axis=0, axis_index_groups=token_groups, tiled=True
+            sent, everywhere, split_axis=0, concat_axis=0, axis_index_groups=token_groups, tiled=True
         )
         return normed, rows
 
@@ -135,7 +145,7 @@
     hidden_other = hidden_units(rows, gate_other, up_other)
     part = down_part(hidden, hidden_other, w_down[0], down_other)
     returned = lax.all_to_all(
-        part, "expert", split_axis=0, concat_axis=0, axis_index_groups=token_groups, tiled=True
+        part, everywhere, split_axis=0, concat_axis=0, axis_index_groups=token_groups, tiled=True
     )
     mixture = product(spread, returned)
 

time: 121 us -> 106 us (0.88)
  the two profiles are of different devices: /device:TPU:1 before, /device:TPU:256 now
where the time goes in v3:
time: 106 us; the launch traced here: 105 us
  blocking collectives  36.3 us (34%)
  waiting for transfers between devices  27.7 us (26%)
  starting transfers between devices  15.8 us (15%)
  Pallas kernels  10.8 us (10%)
  matrix products  7.19 us (7%)
  other arithmetic  5.66 us (5%)
  local copies, waits for them, and re-layouts  1.44 us (1%)
    all_to_all x1, blocking collectives, dispatch(): lax.all_to_all(sent, everywhere, split_axis=0, concat_axis=0, axis_index_...  36.3 us
    all_to_all x1, waiting for transfers between devices, local(): lax.all_to_all(part, everywhere, split_axis=0, concat_axis=0, axis_index_...  26 us
    pallas_call x2, Pallas kernels, hidden_units(): pl.pallas_call(hidden_kernel, grid=(steps,), out_shape=jax.ShapeDtypeStru...  7.45 us
    dot_general x4, matrix products, product(): return jnp.dot(left, right, preferred_element_type=jnp.float32)  7.19 us
    all_to_all x1, starting transfers between devices, local(): lax.all_to_all(part, everywhere, split_axis=0, concat_axis=0, axis_index_...  4.48 us
    ppermute x1, starting transfers between devices, local(): gate_other = lax.ppermute(w_gate[0], everywhere, swap)  3.4 us
    ppermute x1, starting transfers between devices, local(): down_other = lax.ppermute(w_down[0], everywhere, swap)  3.4 us
    pallas_call x1, Pallas kernels, down_part(): pl.pallas_call(down_kernel, grid=(steps,), out_shape=jax.ShapeDtypeStruct...  3.36 us
  transfers between devices with their start and end apart: 5, of which 2 were waited for; matrix products, arithmetic and copies ran while one was open for 10% of the time, Pallas kernels for 7%

profile of v3, /device:TPU:256, one launch (start us, length us, event | category | flops | bytes accessed | tf_op | source)
XLA Modules:
  0.0 105.1 jit_solution(10591059180929802554)
XLA Ops:
  0.0 0.0 copy-start
  0.0 2.0 %collective-permute-start = (bf16[192,2048]{1,0:T(8,128)(2,1)}, bf16[192,2048]{1,0:T(8,128)(2,1)S(1)}, u32[]{:S(2)}, u32[]{:S(2)}) collective-permute-start(bf16[192,2048]{1,0:T(8,128)(2,1)} %bitcast.36), channel_id=1, source_target_pairs={{0,16},{16,32},{32,48},{48,64},{64,80},{80,96},{96,112},{112,128},... | collective-permute-start | bytes 2359304 | tf_op jit(solution)/shard_map/ppermute | solution.py:15
  2.1 3.4 %collective-permute-start.1 = (bf16[2048,256]{1,0:T(8,128)(2,1)}, bf16[2048,256]{1,0:T(8,128)(2,1)}, u32[]{:S(2)}, u32[]{:S(2)}) collective-permute-start(bf16[2048,256]{1,0:T(8,128)(2,1)} %bitcast.25), channel_id=1, source_target_pairs={{0,1},{1,0},{2,3},{3,2},{4,5},{5,4},{6,7},{7,6},{8,9},{9,8},{10,11... | collective-permute-start | bytes 3145736 | tf_op jit(solution)/shard_map/ppermute | solution.py:114
  5.5 2.4 %collective-permute-start.2 = (bf16[2048,256]{1,0:T(8,128)(2,1)}, bf16[2048,256]{1,0:T(8,128)(2,1)}, u32[]{:S(2)}, u32[]{:S(2)}) collective-permute-start(bf16[2048,256]{1,0:T(8,128)(2,1)} %bitcast.27), channel_id=1, source_target_pairs={{0,1},{1,0},{2,3},{3,2},{4,5},{5,4},{6,7},{7,6},{8,9},{9,8},{10,11... | collective-permute-start | bytes 3145736 | tf_op jit(solution)/shard_map/ppermute | solution.py:115
  7.9 3.4 %collective-permute-start.3 = (bf16[256,2048]{1,0:T(8,128)(2,1)}, bf16[256,2048]{1,0:T(8,128)(2,1)S(1)}, u32[]{:S(2)}, u32[]{:S(2)}) collective-permute-start(bf16[256,2048]{1,0:T(8,128)(2,1)} %bitcast.23), channel_id=1, source_target_pairs={{0,1},{1,0},{2,3},{3,2},{4,5},{5,4},{6,7},{7,6},{8,9},{9,8},{10,11... | collective-permute-start | bytes 3145736 | tf_op jit(solution)/shard_map/ppermute | solution.py:116
  11.3 1.0 fusion.3
  12.3 0.7 multiply_add_fusion
  13.0 0.1 compare_convert_fusion
  13.2 1.7 %collective-permute-done = bf16[192,2048]{1,0:T(8,128)(2,1)S(1)} collective-permute-done((bf16[192,2048]{1,0:T(8,128)(2,1)}, bf16[192,2048]{1,0:T(8,128)(2,1)S(1)}, u32[]{:S(2)}, u32[]{:S(2)}) %collective-permute-start) | collective-permute-done | bytes 786464 | tf_op jit(solution)/shard_map/ppermute | solution.py:15
  14.9 1.0 broadcast_select_fusion
  15.8 0.0 copy-done.6
  15.8 42.1 %conditional.1 = (bf16[192,2048]{1,0:T(8,128)(2,1)}, bf16[576,2048]{1,0:T(8,128)(2,1)S(1)}) conditional(s32[]{:T(128)} %convert_element_type.40, bf16[192,2048]{1,0:T(8,128)(2,1)} %broadcast_select_fusion, (bf16[192,2048]{1,0:T(8,128)(2,1)}, bf16[1,2048]{1,0:T(2,128)(2,1)S(1)}, bf16[576,192]{1,0:T(8,128)(2,1)S(1)}) %tuple.17), branch_computations={%region_1.2_spmd, %region_2.4_spmd} | conditional | flops 456919232 | bytes 10468368 | solution.py:142
  15.8 1.5 %fusion = f32[192]{0:T(256)S(1)} fusion(bf16[192,2048]{1,0:T(8,128)(2,1)} %get-tuple-element.12), kind=kLoop, calls=%fused_computation.3 | loop fusion | flops 1179456 | bytes 787200 | tf_op jit(solution)/shard_map/cond/branch_1_fun/reduce_sum | solution.py:20
  17.4 2.3 %fusion.2 = bf16[192,2048]{1,0:T(8,128)(2,1)} fusion(bf16[192,2048]{1,0:T(8,128)(2,1)} %get-tuple-element.12, f32[2048]{0:T(1024)S(1)} %bitcast.32, f32[192]{0:T(256)S(1)} %add_rsqrt_fusion), kind=kLoop, calls=%fused_computation.5 | loop fusion | flops 1572864 | bytes 1581824 | tf_op jit(solution)/shard_map/cond/branch_1_fun/convert_element_type | solution.py:21
  19.6 1.9 %convolution_convert_fusion = bf16[2048,576]{0,1:T(8,128)(2,1)S(1)} fusion(bf16[576,192]{1,0:T(8,128)(2,1)S(1)} %get-tuple-element.14, bf16[192,2048]{1,0:T(8,128)(2,1)} %fusion.2), kind=kOutput, calls=%fused_computation | convolution fusion | flops 454164480 | bytes 3366912 | tf_op jit(solution)/shard_map/cond/branch_1_fun/dot_general | solution.py:25
  21.6 36.3 %all_to_all.21 = bf16[8,72,2048]{2,1,0:T(8,128)(2,1)S(1)} all-to-all(bf16[8,72,2048]{2,1,0:T(8,128)(2,1)S(1)} %bitcast.31), channel_id=1, replica_groups={{0,3,4,7,8,11,12,15},{1,2,5,6,9,10,13,14},{16,17,20,21,24,25,28,29},{18..., dimensions={0} | all-to-all | bytes 4718592 | tf_op jit(solution)/shard_map/cond/branch_1_fun/all_to_all | solution.py:132
  57.9 1.4 %copy-done.4 = bf16[576,2048]{1,0:T(8,128)(2,1)} copy-done((bf16[576,2048]{1,0:T(8,128)(2,1)}, bf16[576,2048]{1,0:T(8,128)(2,1)S(1)}, u32[]{:S(2)}) %copy-start.4) | copy-done | bytes 2359320
  59.3 0.0 copy-done.2
  59.3 0.0 copy-done.3
  59.3 3.8 %shard_map.83.hidden_ref = bf16[576,256]{1,0:T(8,128)(2,1)S(1)} custom-call(bf16[576,2048]{1,0:T(8,128)(2,1)} %copy-done.4, bf16[2048,256]{1,0:T(8,128)(2,1)S(1)} %bitcast.26, bf16[2048,256]{1,0:T(8,128)(2,1)S(1)} %bitcast.28), custom_call_target="tpu_custom_call" | custom-call | flops 1207959552 | bytes 4751360 | tf_op jit(solution)/shard_map/pallas_call | solution.py:43
  63.1 0.0 copy-start.1
  63.1 0.0 collective-permute-done.1.gate_ref
  63.2 0.0 collective-permute-done.2.up_ref
  63.2 0.0 copy-done.5
  63.2 3.6 %shard_map.84.other_ref = bf16[576,256]{1,0:T(8,128)(2,1)S(1)} custom-call(bf16[576,2048]{1,0:T(8,128)(2,1)S(1)} %copy-done.5, bf16[2048,256]{1,0:T(8,128)(2,1)} %collective-permute-done.1.gate_ref, bf16[2048,256]{1,0:T(8,128)(2,1)} %collective-permute-done.2.up_ref), custom_call_target="tpu_custom_call" | custom-call | flops 1207959552 | bytes 4751360 | tf_op jit(solution)/shard_map/pallas_call | solution.py:43
  66.8 0.0 collective-permute-done.3.down_other_ref
  66.8 0.0 copy-done.1
  66.8 3.4 %shard_map.85 = bf16[576,2048]{1,0:T(8,128)(2,1)} custom-call(bf16[576,256]{1,0:T(8,128)(2,1)S(1)} %shard_map.83.hidden_ref, bf16[576,256]{1,0:T(8,128)(2,1)S(1)} %shard_map.84.other_ref, bf16[256,2048]{1,0:T(8,128)(2,1)S(1)} %bitcast.24, bf16[256,2048]{1,0:T(8,128)(2,1)S(1)} %collective-permute-done.3.down_other_ref), custom_call_target="tpu_custom_call" | custom-call | flops 1207959552 | bytes 5046272 | tf_op jit(solution)/shard_map/pallas_call | solution.py:72
  70.2 4.5 %all-to-all-start.1 = ((bf16[8,72,2048]{2,1,0:T(8,128)(2,1)}), bf16[8,72,2048]{2,1,0:T(8,128)(2,1)S(1)}, u32[]{:S(2)}, u32[]{:S(2)}) async-start(bf16[8,72,2048]{2,1,0:T(8,128)(2,1)} %bitcast.10), calls=%async_computation.1 | async-start | bytes 4718592 | tf_op jit(solution)/shard_map/all_to_all | solution.py:147
  74.7 1.5 %fusion.22 = (f32[192]{0:T(256)S(1)}, f32[192,4]{0,1:T(4,128)S(1)}) fusion(bf16[192,2048]{1,0:T(8,128)(2,1)} %get-tuple-element.17, bf16[1,2048,4]{1,2,0:T(4,128)(2,1)S(1)} %copy-done), kind=kOutput, calls=%fused_computation.39 | convolution fusion | flops 3146304 | bytes 806656 | tf_op jit(solution)/shard_map/dot_general | solution.py:25
  76.2 26.0 %all-to-all-done.1 = bf16[8,72,2048]{2,1,0:T(8,128)(2,1)S(1)} async-done(((bf16[8,72,2048]{2,1,0:T(8,128)(2,1)}), bf16[8,72,2048]{2,1,0:T(8,128)(2,1)S(1)}, u32[]{:S(2)}, u32[]{:S(2)}) %all-to-all-start.1) | async-done | bytes 2359328 | tf_op jit(solution)/shard_map/all_to_all | solution.py:147
  102.2 2.9 %fusion.4 = bf16[1,192,2048]{2,1,0:T(8,128)(2,1)} fusion(bf16[192,2048]{1,0:T(8,128)(2,1)} %broadcast_select_fusion, bf16[576,2048]{1,0:T(8,128)(2,1)S(1)} %bitcast.30, f32[192]{0:T(256)S(1)} %fusion.17, s32[576]{0:T(1024)S(1)} %iota_subtract_fusion, s32[192]{0:T(256)S(1)} %multiply_add_fusion), kind=kOutput, calls=%fused_computation.12 | convolution fusion | flops 454668288 | bytes 3936000 | tf_op jit(solution)/shard_map/dot_general | solution.py:25
  (13 shorter events, 0.1 us)
Async XLA Ops:
  0.0 74.7 %copy-start = (bf16[1,2048,4]{1,2,0:T(4,128)(2,1)S(1)}, bf16[1,2048,4]{1,2,0:T(4,128)(2,1)}, u32[]{:S(2)}) copy-start(bf16[1,2048,4]{1,2,0:T(4,128)(2,1)} %param.13) | copy-start | bytes 49156
  0.0 15.8 %copy-start.6 = (bf16[1,2048]{1,0:T(2,128)(2,1)S(1)}, bf16[1,2048]{1,0:T(2,128)(2,1)}, u32[]{:S(2)}) copy-start(bf16[1,2048]{1,0:T(2,128)(2,1)} %param.12) | copy-start | bytes 12292
  0.0 14.8 %collective-permute-start = (bf16[192,2048]{1,0:T(8,128)(2,1)}, bf16[192,2048]{1,0:T(8,128)(2,1)S(1)}, u32[]{:S(2)}, u32[]{:S(2)}) collective-permute-start(bf16[192,2048]{1,0:T(8,128)(2,1)} %bitcast.36), channel_id=1, source_target_pairs={{0,16},{16,32},{32,48},{48,64},{64,80},{80,96},{96,112},{112,128},... | collective-permute-start | bytes 2359304 | tf_op jit(solution)/shard_map/ppermute | solution.py:15
  2.1 61.1 %collective-permute-start.1 = (bf16[2048,256]{1,0:T(8,128)(2,1)}, bf16[2048,256]{1,0:T(8,128)(2,1)}, u32[]{:S(2)}, u32[]{:S(2)}) collective-permute-start(bf16[2048,256]{1,0:T(8,128)(2,1)} %bitcast.25), channel_id=1, source_target_pairs={{0,1},{1,0},{2,3},{3,2},{4,5},{5,4},{6,7},{7,6},{8,9},{9,8},{10,11... | collective-permute-start | bytes 3145736 | tf_op jit(solution)/shard_map/ppermute | solution.py:114
  5.5 57.7 %collective-permute-start.2 = (bf16[2048,256]{1,0:T(8,128)(2,1)}, bf16[2048,256]{1,0:T(8,128)(2,1)}, u32[]{:S(2)}, u32[]{:S(2)}) collective-permute-start(bf16[2048,256]{1,0:T(8,128)(2,1)} %bitcast.27), channel_id=1, source_target_pairs={{0,1},{1,0},{2,3},{3,2},{4,5},{5,4},{6,7},{7,6},{8,9},{9,8},{10,11... | collective-permute-start | bytes 3145736 | tf_op jit(solution)/shard_map/ppermute | solution.py:115
  7.9 58.9 %collective-permute-start.3 = (bf16[256,2048]{1,0:T(8,128)(2,1)}, bf16[256,2048]{1,0:T(8,128)(2,1)S(1)}, u32[]{:S(2)}, u32[]{:S(2)}) collective-permute-start(bf16[256,2048]{1,0:T(8,128)(2,1)} %bitcast.23), channel_id=1, source_target_pairs={{0,1},{1,0},{2,3},{3,2},{4,5},{5,4},{6,7},{7,6},{8,9},{9,8},{10,11... | collective-permute-start | bytes 3145736 | tf_op jit(solution)/shard_map/ppermute | solution.py:116
  15.8 43.5 %copy-start.2 = (bf16[1,2048,256]{2,1,0:T(8,128)(2,1)S(1)}, bf16[1,2048,256]{2,1,0:T(8,128)(2,1)}, u32[]{:S(2)}) copy-start(bf16[1,2048,256]{2,1,0:T(8,128)(2,1)} %param.14) | copy-start | bytes 3145732
  15.8 43.5 %copy-start.3 = (bf16[1,2048,256]{2,1,0:T(8,128)(2,1)S(1)}, bf16[1,2048,256]{2,1,0:T(8,128)(2,1)}, u32[]{:S(2)}) copy-start(bf16[1,2048,256]{2,1,0:T(8,128)(2,1)} %param.15) | copy-start | bytes 3145732
  57.9 1.4 %copy-start.4 = (bf16[576,2048]{1,0:T(8,128)(2,1)}, bf16[576,2048]{1,0:T(8,128)(2,1)S(1)}, u32[]{:S(2)}) copy-start(bf16[576,2048]{1,0:T(8,128)(2,1)S(1)} %get-tuple-element.18.rows_ref) | copy-start | bytes 7077892
  59.3 3.9 %copy-start.5 = (bf16[576,2048]{1,0:T(8,128)(2,1)S(1)}, bf16[576,2048]{1,0:T(8,128)(2,1)}, u32[]{:S(2)}) copy-start(bf16[576,2048]{1,0:T(8,128)(2,1)} %copy-done.4) | copy-start | bytes 7077892
  63.1 3.7 %copy-start.1 = (bf16[1,256,2048]{2,1,0:T(8,128)(2,1)S(1)}, bf16[1,256,2048]{2,1,0:T(8,128)(2,1)}, u32[]{:S(2)}) copy-start(bf16[1,256,2048]{2,1,0:T(8,128)(2,1)} %param.16) | copy-start | bytes 3145732
  70.2 6.0 %copy-start.7 = (s32[1,192,1]{1,2,0:T(1,128)S(1)}, s32[1,192,1]{1,2,0:T(1,128)}, u32[]{:S(2)}) copy-start(s32[1,192,1]{1,2,0:T(1,128)} %param.17) | copy-start | bytes 2308
  70.2 32.0 %all-to-all-start.1 = ((bf16[8,72,2048]{2,1,0:T(8,128)(2,1)}), bf16[8,72,2048]{2,1,0:T(8,128)(2,1)S(1)}, u32[]{:S(2)}, u32[]{:S(2)}) async-start(bf16[8,72,2048]{2,1,0:T(8,128)(2,1)} %bitcast.10), calls=%async_computation.1 | async-start | bytes 4718592 | tf_op jit(solution)/shard_map/all_to_all | solution.py:147

commit v4 on v3

v4 whole, which is shorter than its diff:
```python
import jax
import jax.numpy as jnp
from jax import lax
from jax.experimental import pallas as pl
from jax.experimental.pallas import tpu as pltpu
from jax.sharding import PartitionSpec as P

CAP = 72
VMEM_BYTES = 48 * 1024 * 1024
HIDDEN_VMEM_BYTES = 52 * 1024 * 1024


def passed_along(block, axis, distance):
    devices = range(lax.axis_size(axis))
    route = [(i - distance, i) for i in devices if i - distance in devices]
    return lax.ppermute(block, axis, route)


def product(left, right):
    return jnp.dot(left, right, preferred_element_type=jnp.float32)


def anywhere():
    return pl.BlockSpec(memory_space=pl.ANY)


def column_of(row, zero):
    size = row.shape[1]
    across, down = (lax.broadcasted_iota(jnp.int32, (size, size), d) for d in (1, 0))
    return jnp.sum(jnp.where(across == down, row, zero), axis=1, keepdims=True)


def front_kernel(first_ref, small_ref, arrived_ref, entering_ref, arriving_ref, gate_ref, place_ref, sent_ref, sent, out_sems):
    slots, features = sent.shape
    tokens = arrived_ref.shape[0]
    experts = small_ref.shape[0] - 2
    steps = out_sems.shape[0]
    block = slots // steps
    span = 2 * CAP

    router = small_ref[:experts, :].astype(jnp.bfloat16)
    gain = small_ref[experts : experts + 1, :]
    chosen = small_ref[experts + 1 :, :tokens].astype(jnp.int32)
    assigned = chosen == lax.broadcasted_iota(jnp.int32, (experts, tokens), 0)
    across, down = (lax.broadcasted_iota(jnp.int32, (tokens, tokens), d) for d in (1, 0))
    ranks = product(assigned.astype(jnp.bfloat16), (down < across).astype(jnp.bfloat16))
    rank = jnp.sum(jnp.where(assigned, ranks, 0.0), axis=0, keepdims=True).astype(jnp.int32)
    place = rank + chosen * span
    place_ref[...] = column_of(place, 0)
    slot = lax.broadcasted_iota(jnp.int32, (slots, tokens), 0)
    row_slot = jnp.where(slot % span < CAP, slot, slot - CAP)
    select = (place == row_slot).astype(jnp.bfloat16)

    arriving = jnp.where(first_ref[0] == 1, entering_ref[...], arrived_ref[...])
    arriving_ref[...] = arriving
    values = arriving.astype(jnp.float32)
    written = []
    scaling = lax.rsqrt(jnp.mean(values * values, axis=-1, keepdims=True) + 1e-06)
    normed = (values * scaling * gain).astype(jnp.bfloat16)
    for step in range(steps):
        here = pl.ds(step * block, block)
        sent[here, :] = product(select[step * block : (step + 1) * block], normed).astype(jnp.bfloat16)
        copy = pltpu.make_async_copy(sent.at[here], sent_ref.at[here], out_sems.at[step])
        copy.start()
        written.append(copy)
    logits = lax.dot_general(router, normed, (((1,), (1,)), ((), ())), preferred_element_type=jnp.float32)
    weights = jnp.exp(logits)
    probability = weights / jnp.sum(weights, axis=0, keepdims=True)
    gate_ref[...] = column_of(jnp.sum(jnp.where(assigned, probability, 0.0), axis=0, keepdims=True), 0.0)
    for copy in written:
        copy.wait()


def front(first, small, arrived, entering, slots, steps=2):
    tokens, features = entering.shape
    vmem = pl.BlockSpec(memory_space=pltpu.VMEM)
    return pl.pallas_call(
        front_kernel,
        out_shape=(
            jax.ShapeDtypeStruct((tokens, features), jnp.bfloat16),
            jax.ShapeDtypeStruct((tokens, 1), jnp.float32),
            jax.ShapeDtypeStruct((tokens, 1), jnp.int32),
            jax.ShapeDtypeStruct((slots, features), jnp.bfloat16),
        ),
        in_specs=[pl.BlockSpec(memory_space=pltpu.SMEM)] + [vmem] * 3,
        out_specs=(vmem, vmem, vmem, anywhere()),
        scratch_shapes=[
            pltpu.VMEM((slots, features), jnp.bfloat16),
            pltpu.SemaphoreType.DMA((steps,)),
        ],
        compiler_params=pltpu.CompilerParams(vmem_limit_bytes=VMEM_BYTES),
        cost_estimate=pl.CostEstimate(
            flops=40 * slots * tokens * features, bytes_accessed=2 * features * (3 * tokens + slots), transcendentals=tokens
        ),
    )(first, small, arrived, entering)


def hidden_kernel(rows_ref, gate_ref, up_ref, gate_other_ref, up_other_ref, hidden_ref, rows, gate_up, in_sems):
    count, features = rows.shape
    units = gate_ref.shape[1]
    steps = 2
    block = count // steps

    def fetch(source, target, index):
        copy = pltpu.make_async_copy(source, target, in_sems.at[index])
        copy.start()
        return copy

    first, second = pl.ds(0, units), pl.ds(units, units)
    row_copy = fetch(rows_ref, rows, 0)
    panels = [
        (fetch(gate, gate_up.at[i, :, first], 1 + 2 * i), fetch(up, gate_up.at[i, :, second], 2 + 2 * i))
        for i, (gate, up) in enumerate(((gate_ref, up_ref), (gate_other_ref, up_other_ref)))
    ]
    row_copy.wait()
    for i, copies in enumerate(panels):
        for copy in copies:
            copy.wait()

        def multiply(step, carry):
            here = pl.ds(pl.multiple_of(step * block, block), block)
            both = product(rows[here, :], gate_up[i])
            units_here = jax.nn.silu(both[:, :units]) * both[:, units:]
            hidden_ref[here, i * units : (i + 1) * units] = units_here.astype(jnp.bfloat16)
            return carry

        lax.fori_loop(0, steps, multiply, 0)


def hidden_units(rows, gate, up, gate_other, up_other):
    count, features = rows.shape
    units = gate.shape[1]
    return pl.pallas_call(
        hidden_kernel,
        out_shape=jax.ShapeDtypeStruct((count, 2 * units), jnp.bfloat16),
        in_specs=[anywhere()] * 5,
        out_specs=pl.BlockSpec(memory_space=pltpu.VMEM),
        scratch_shapes=[
            pltpu.VMEM((count, features), jnp.bfloat16),
            pltpu.VMEM((2, features, 2 * units), jnp.bfloat16),
            pltpu.SemaphoreType.DMA((5,)),
        ],
        compiler_params=pltpu.CompilerParams(vmem_limit_bytes=HIDDEN_VMEM_BYTES),
        cost_estimate=pl.CostEstimate(
            flops=8 * count * features * units,
            bytes_accessed=2 * (count * features + 4 * features * units),
            transcendentals=2 * count * units,
        ),
    )(rows, gate, up, gate_other, up_other)


def down_kernel(hidden_ref, down_ref, down_other_ref, part_ref):
    units = down_ref.shape[0]
    total = product(hidden_ref[:, :units], down_ref[...])
    total += product(hidden_ref[:, units:], down_other_ref[...])
    part_ref[...] = total.astype(part_ref.dtype)


def down_part(hidden, down, down_other, steps=4):
    count = hidden.shape[0]
    units, features = down.shape
    block = features // steps
    return pl.pallas_call(
        down_kernel,
        grid=(steps,),
        out_shape=jax.ShapeDtypeStruct((count, features), jnp.bfloat16),
        in_specs=[
            pl.BlockSpec((count, 2 * units), lambda i: (0, 0)),
            pl.BlockSpec((units, block), lambda i: (0, i)),
            pl.BlockSpec((units, block), lambda i: (0, i)),
        ],
        out_specs=pl.BlockSpec((count, block), lambda i: (0, i)),
        compiler_params=pltpu.CompilerParams(vmem_limit_bytes=VMEM_BYTES),
        cost_estimate=pl.CostEstimate(
            flops=4 * count * features * units,
            bytes_accessed=2 * (count * (features + 2 * units) + 2 * features * units),
            transcendentals=0,
        ),
    )(hidden, down, down_other)


def combine_kernel(place_ref, returned_ref, arriving_ref, gate_ref, mixed_ref):
    tokens, slots = place_ref.shape[0], returned_ref.shape[0]
    slot = lax.broadcasted_iota(jnp.int32, (tokens, slots), 1)
    row_slot = jnp.where(slot % (2 * CAP) < CAP, slot, slot - CAP)
    spread = (place_ref[...] == row_slot).astype(jnp.bfloat16)
    mixture = product(spread, returned_ref[...])
    mixed = arriving_ref[...].astype(jnp.float32) + gate_ref[...] * mixture
    mixed_ref[0] = mixed.astype(mixed_ref.dtype)


def combine(place, returned, arriving, gate_value, steps=1):
    tokens, features = arriving.shape
    slots = returned.shape[0]
    block = features // steps
    return pl.pallas_call(
        combine_kernel,
        grid=(steps,),
        out_shape=jax.ShapeDtypeStruct((1, tokens, features), jnp.bfloat16),
        in_specs=[
            pl.BlockSpec((tokens, 1), lambda i: (0, 0)),
            pl.BlockSpec((slots, block), lambda i: (0, i)),
            pl.BlockSpec((tokens, block), lambda i: (0, i)),
            pl.BlockSpec((tokens, 1), lambda i: (0, 0)),
        ],
        out_specs=pl.BlockSpec((1, tokens, block), lambda i: (0, 0, i)),
        compiler_params=pltpu.CompilerParams(vmem_limit_bytes=VMEM_BYTES),
        cost_estimate=pl.CostEstimate(
            flops=2 * slots * tokens * features, bytes_accessed=2 * features * (2 * tokens + slots), transcendentals=0
        ),
    )(place, returned, arriving, gate_value)


def local(held, entering, norm_gain, router, w_gate, w_up, w_down, expert_ids):
    experts = router.shape[2]
    group = lax.axis_size("expert")
    panels = group // experts
    tokens, features = entering.shape
    sections = lax.axis_size("section")
    everywhere = ("section", "expert")
    near, mirrored = (lambda x: x ^ 1), (lambda x: panels - 1 - x)
    swap, token_groups = [], []
    for section in range(sections):
        weight_partner, token_partner = (near, mirrored) if section % 2 == 0 else (mirrored, near)
        start = section * group
        for i in range(group):
            swap.append((start + i, start + i - i % panels + weight_partner(i % panels)))
        for x in range(panels):
            if x < token_partner(x):
                pair = (x, token_partner(x))
                token_groups.append([start + e * panels + c for e in range(experts) for c in pair])
    span = 2 * CAP
    slots = experts * span

    gate_other = lax.ppermute(w_gate[0], everywhere, swap)
    up_other = lax.ppermute(w_up[0], everywhere, swap)
    down_other = lax.ppermute(w_down[0], everywhere, swap)
    arrived = passed_along(held[0], "section", 1)

    first = (lax.axis_index("section") == 0).astype(jnp.int32).reshape(1)

    chosen = jnp.pad(expert_ids[0].T.astype(jnp.float32), ((0, 0), (0, features - tokens)))
    small = jnp.concatenate([router[0].T.astype(jnp.float32), norm_gain.astype(jnp.float32), chosen], axis=0)

    def exchange(blocks):
        return lax.all_to_all(
            blocks, everywhere, split_axis=0, concat_axis=0, axis_index_groups=token_groups, tiled=True
        )

    arriving, gate_value, place, sent = front(
        first, small, arrived, jnp.where(first[0] == 1, entering, jnp.zeros_like(entering)), slots
    )
    here = lax.axis_index("section") < sections
    rows = lax.cond(here, exchange, jnp.zeros_like, sent)
    hidden = hidden_units(rows, w_gate[0], w_up[0], gate_other, up_other)
    part = down_part(hidden, w_down[0], down_other)
    return combine(place, exchange(part), arriving, gate_value)


def solution(mesh):
    placed = (
        P("section", "expert", None),
        P("expert", None),
        P("section", None),
        P("section", None, None),
        P("section", None, "expert"),
        P("section", None, "expert"),
        P("section", "expert", None),
        P("section", "expert", None),
    )
    return jax.shard_map(
        local, mesh=mesh, in_specs=placed, out_specs=P("section", "expert", None), check_vma=False
    )
```

time: 106 us -> 97.1 us (0.916)
  the two profiles are of different devices: /device:TPU:256 before, /device:TPU:224 now
where the time goes in v4:
time: 97.1 us; the launch traced here: 96.6 us
  blocking collectives  71.5 us (74%)
  Pallas kernels  11.5 us (12%)
  starting transfers between devices  11.2 us (12%)
  other arithmetic  2.2 us (2%)
    all_to_all x2, blocking collectives, exchange(): lax.all_to_all(blocks, everywhere, split_axis=0, concat_axis=0, axis_inde...  71.5 us
    pallas_call x1, Pallas kernels, hidden_units(): pl.pallas_call(hidden_kernel, out_shape=jax.ShapeDtypeStruct((count, 2 *...  5.2 us
    ppermute x1, starting transfers between devices, local(): gate_other = lax.ppermute(w_gate[0], everywhere, swap)  3.4 us
    ppermute x1, starting transfers between devices, local(): down_other = lax.ppermute(w_down[0], everywhere, swap)  3.4 us
    ppermute x1, starting transfers between devices, local(): up_other = lax.ppermute(w_up[0], everywhere, swap)  2.45 us
    pallas_call x1, Pallas kernels, front(): pl.pallas_call(front_kernel, out_shape=(jax.ShapeDtypeStruct((tokens, fea...  2.4 us
    pallas_call x1, Pallas kernels, down_part(): pl.pallas_call(down_kernel, grid=(steps,), out_shape=jax.ShapeDtypeStruct...  2.22 us
  transfers between devices with their start and end apart: 4, of which 1 were waited for; matrix products, arithmetic and copies ran while one was open for 2% of the time, Pallas kernels for 8%

profile of v4, /device:TPU:224, one launch (start us, length us, event | category | flops | bytes accessed | tf_op | source)
XLA Modules:
  0.0 96.6 jit_solution(1686272666072421510)
XLA Ops:
  0.0 1.9 %collective-permute-start = (bf16[192,2048]{1,0:T(8,128)(2,1)}, bf16[192,2048]{1,0:T(8,128)(2,1)S(1)}, u32[]{:S(2)}, u32[]{:S(2)}) collective-permute-start(bf16[192,2048]{1,0:T(8,128)(2,1)} %bitcast.26), channel_id=1, source_target_pairs={{0,16},{16,32},{32,48},{48,64},{64,80},{80,96},{96,112},{112,128},... | collective-permute-start | bytes 2359304 | tf_op jit(solution)/shard_map/ppermute | solution.py:16
  1.9 3.4 %collective-permute-start.1 = (bf16[2048,256]{1,0:T(8,128)(2,1)}, bf16[2048,256]{1,0:T(8,128)(2,1)}, u32[]{:S(2)}, u32[]{:S(2)}) collective-permute-start(bf16[2048,256]{1,0:T(8,128)(2,1)} %bitcast.20), channel_id=1, source_target_pairs={{0,1},{1,0},{2,3},{3,2},{4,5},{5,4},{6,7},{7,6},{8,9},{9,8},{10,11... | collective-permute-start | bytes 3145736 | tf_op jit(solution)/shard_map/ppermute | solution.py:235
  5.3 2.4 %collective-permute-start.2 = (bf16[2048,256]{1,0:T(8,128)(2,1)}, bf16[2048,256]{1,0:T(8,128)(2,1)}, u32[]{:S(2)}, u32[]{:S(2)}) collective-permute-start(bf16[2048,256]{1,0:T(8,128)(2,1)} %bitcast.24), channel_id=1, source_target_pairs={{0,1},{1,0},{2,3},{3,2},{4,5},{5,4},{6,7},{7,6},{8,9},{9,8},{10,11... | collective-permute-start | bytes 3145736 | tf_op jit(solution)/shard_map/ppermute | solution.py:236
  7.8 3.4 %collective-permute-start.3 = (bf16[256,2048]{1,0:T(8,128)(2,1)}, bf16[256,2048]{1,0:T(8,128)(2,1)S(1)}, u32[]{:S(2)}, u32[]{:S(2)}) collective-permute-start(bf16[256,2048]{1,0:T(8,128)(2,1)} %bitcast.18), channel_id=1, source_target_pairs={{0,1},{1,0},{2,3},{3,2},{4,5},{5,4},{6,7},{7,6},{8,9},{9,8},{10,11... | collective-permute-start | bytes 3145736 | tf_op jit(solution)/shard_map/ppermute | solution.py:237
  11.2 0.7 convert_bitcast_fusion
  11.9 0.7 convert_bitcast_fusion.1
  12.6 0.7 convert_element_type.38
  13.3 0.1 broadcast_select_fusion.entering_ref
  13.4 0.1 collective-permute-done.arrived_ref
  13.5 2.4 %shard_map.82 = (bf16[192,2048]{1,0:T(8,128)(2,1)S(1)}, f32[192,1]{1,0:T(8,128)S(1)}, s32[192,1]{1,0:T(8,128)S(1)}, bf16[576,2048]{1,0:T(8,128)(2,1)}) custom-call(s32[1]{0:T(128)} %bitcast.2.first_ref, f32[6,2048]{1,0:T(8,128)S(1)} %select_maximum_fusion.small_ref, bf16[192,2048]{1,0:T(8,128)(2,1)S(1)} %collective-permute-done.arrived_ref, ...), custom_call_target="tpu_custom_call" | custom-call | flops 9059696640 | bytes 4718592 | tf_op jit(solution)/shard_map/pallas_call | solution.py:77
  15.9 0.0 copy-start.1
  15.9 39.4 %conditional.1 = (bf16[576,2048]{1,0:T(8,128)(2,1)}) conditional(s32[]{:T(128)} %convert_element_type.41, () %tuple.11, bf16[576,2048]{1,0:T(8,128)(2,1)} %get-tuple-element.14), branch_computations={%region_0.1_spmd, %region_1.2_spmd} | conditional | bytes 4718600 | solution.py:254
  15.9 39.4 %all_to_all.20 = bf16[8,72,2048]{2,1,0:T(8,128)(2,1)} all-to-all(bf16[8,72,2048]{2,1,0:T(8,128)(2,1)} %bitcast.23), channel_id=1, replica_groups={{0,3,4,7,8,11,12,15},{1,2,5,6,9,10,13,14},{16,17,20,21,24,25,28,29},{18..., dimensions={0} | all-to-all | bytes 4718592 | tf_op jit(solution)/shard_map/cond/branch_1_fun/all_to_all | solution.py:246
  55.3 0.0 copy-start
  55.3 0.0 collective-permute-done.1.gate_other_ref
  55.3 0.0 collective-permute-done.2.up_other_ref
  55.3 0.0 copy-done.1
  55.3 5.2 %shard_map.83.hidden_ref = bf16[576,512]{1,0:T(8,128)(2,1)S(1)} custom-call(bf16[576,2048]{1,0:T(8,128)(2,1)} %get-tuple-element.17.rows_ref, bf16[2048,256]{1,0:T(8,128)(2,1)S(1)} %bitcast.21, bf16[2048,256]{1,0:T(8,128)(2,1)} %bitcast.25, bf16[2048,256]{1,0:T(8,128)(2,1)} %collective-permute-done.1.gate_other_ref, ...), custom_call_target="tpu_custom_call" | custom-call | flops 2415919104 | bytes 6553600 | tf_op jit(solution)/shard_map/pallas_call | solution.py:133
  60.5 0.0 collective-permute-done.3.down_other_ref
  60.5 0.0 copy-done
  60.5 2.2 %shard_map.84 = bf16[576,2048]{1,0:T(8,128)(2,1)S(1)} custom-call(bf16[576,512]{1,0:T(8,128)(2,1)S(1)} %shard_map.83.hidden_ref, bf16[256,2048]{1,0:T(8,128)(2,1)S(1)} %bitcast.19, bf16[256,2048]{1,0:T(8,128)(2,1)S(1)} %collective-permute-done.3.down_other_ref), custom_call_target="tpu_custom_call" | custom-call | flops 1207959552 | bytes 5046272 | tf_op jit(solution)/shard_map/pallas_call | solution.py:163
  62.8 32.1 %all_to_all.21 = bf16[8,72,2048]{2,1,0:T(8,128)(2,1)S(1)} all-to-all(bf16[8,72,2048]{2,1,0:T(8,128)(2,1)S(1)} %bitcast.16), channel_id=1, replica_groups={{0,3,4,7,8,11,12,15},{1,2,5,6,9,10,13,14},{16,17,20,21,24,25,28,29},{18..., dimensions={0} | all-to-all | bytes 4718592 | tf_op jit(solution)/shard_map/all_to_all | solution.py:246
  94.9 1.7 %shard_map.85 = bf16[1,192,2048]{2,1,0:T(8,128)(2,1)} custom-call(s32[192,1]{1,0:T(8,128)S(1)} %get-tuple-element.13.place_ref, bf16[576,2048]{1,0:T(8,128)(2,1)S(1)} %bitcast.17, bf16[192,2048]{1,0:T(8,128)(2,1)S(1)} %get-tuple-element.15.arriving_ref, f32[192,1]{1,0:T(8,128)S(1)} %get-tuple-element.16.gate_ref), custom_call_target="tpu_custom_call" | custom-call | flops 452984832 | bytes 3932160 | tf_op jit(solution)/shard_map/pallas_call | solution.py:196
  (1 shorter events, 0.0 us)
Async XLA Ops:
  0.0 13.5 %collective-permute-start = (bf16[192,2048]{1,0:T(8,128)(2,1)}, bf16[192,2048]{1,0:T(8,128)(2,1)S(1)}, u32[]{:S(2)}, u32[]{:S(2)}) collective-permute-start(bf16[192,2048]{1,0:T(8,128)(2,1)} %bitcast.26), channel_id=1, source_target_pairs={{0,16},{16,32},{32,48},{48,64},{64,80},{80,96},{96,112},{112,128},... | collective-permute-start | bytes 2359304 | tf_op jit(solution)/shard_map/ppermute | solution.py:16
  1.9 53.4 %collective-permute-start.1 = (bf16[2048,256]{1,0:T(8,128)(2,1)}, bf16[2048,256]{1,0:T(8,128)(2,1)}, u32[]{:S(2)}, u32[]{:S(2)}) collective-permute-start(bf16[2048,256]{1,0:T(8,128)(2,1)} %bitcast.20), channel_id=1, source_target_pairs={{0,1},{1,0},{2,3},{3,2},{4,5},{5,4},{6,7},{7,6},{8,9},{9,8},{10,11... | collective-permute-start | bytes 3145736 | tf_op jit(solution)/shard_map/ppermute | solution.py:235
  5.3 50.0 %collective-permute-start.2 = (bf16[2048,256]{1,0:T(8,128)(2,1)}, bf16[2048,256]{1,0:T(8,128)(2,1)}, u32[]{:S(2)}, u32[]{:S(2)}) collective-permute-start(bf16[2048,256]{1,0:T(8,128)(2,1)} %bitcast.24), channel_id=1, source_target_pairs={{0,1},{1,0},{2,3},{3,2},{4,5},{5,4},{6,7},{7,6},{8,9},{9,8},{10,11... | collective-permute-start | bytes 3145736 | tf_op jit(solution)/shard_map/ppermute | solution.py:236
  7.8 52.8 %collective-permute-start.3 = (bf16[256,2048]{1,0:T(8,128)(2,1)}, bf16[256,2048]{1,0:T(8,128)(2,1)S(1)}, u32[]{:S(2)}, u32[]{:S(2)}) collective-permute-start(bf16[256,2048]{1,0:T(8,128)(2,1)} %bitcast.18), channel_id=1, source_target_pairs={{0,1},{1,0},{2,3},{3,2},{4,5},{5,4},{6,7},{7,6},{8,9},{9,8},{10,11... | collective-permute-start | bytes 3145736 | tf_op jit(solution)/shard_map/ppermute | solution.py:237
  15.9 39.4 %copy-start.1 = (bf16[1,2048,256]{2,1,0:T(8,128)(2,1)S(1)}, bf16[1,2048,256]{2,1,0:T(8,128)(2,1)}, u32[]{:S(2)}) copy-start(bf16[1,2048,256]{2,1,0:T(8,128)(2,1)} %param.14) | copy-start | bytes 3145732
  55.3 5.2 %copy-start = (bf16[1,256,2048]{2,1,0:T(8,128)(2,1)S(1)}, bf16[1,256,2048]{2,1,0:T(8,128)(2,1)}, u32[]{:S(2)}) copy-start(bf16[1,256,2048]{2,1,0:T(8,128)(2,1)} %param.16) | copy-start | bytes 3145732

commit v5 on v4

--- a/solution.py
+++ b/solution.py
@@ -71,7 +71,7 @@
         copy.wait()
 
 
-def front(first, small, arrived, entering, slots, steps=2):
+def front(first, small, arrived, entering, slots, steps=4):
     tokens, features = entering.shape
     vmem = pl.BlockSpec(memory_space=pltpu.VMEM)
     return pl.pallas_call(
@@ -98,7 +98,7 @@
 def hidden_kernel(rows_ref, gate_ref, up_ref, gate_other_ref, up_other_ref, hidden_ref, rows, gate_up, in_sems):
     count, features = rows.shape
     units = gate_ref.shape[1]
-    steps = 2
+    steps = in_sems.shape[0] - 4
     block = count // steps
 
     def fetch(source, target, index):
@@ -107,27 +107,23 @@
         return copy
 
     first, second = pl.ds(0, units), pl.ds(units, units)
-    row_copy = fetch(rows_ref, rows, 0)
-    panels = [
-        (fetch(gate, gate_up.at[i, :, first], 1 + 2 * i), fetch(up, gate_up.at[i, :, second], 2 + 2 * i))
-        for i, (gate, up) in enumerate(((gate_ref, up_ref), (gate_other_ref, up_other_ref)))
-    ]
-    row_copy.wait()
+    blocks = [pl.ds(step * block, block) for step in range(steps)]
+    row_copies = [fetch(rows_ref.at[blocks[0]], rows.at[blocks[0]], 4)]
+    panels = [(fetch(gate_ref, gate_up.at[0, :, first], 0), fetch(up_ref, gate_up.at[0, :, second], 1))]
+    row_copies += [fetch(rows_ref.at[blocks[i]], rows.at[blocks[i]], 4 + i) for i in range(1, steps)]
+    panels += [(fetch(gate_other_ref, gate_up.at[1, :, first], 2), fetch(up_other_ref, gate_up.at[1, :, second], 3))]
     for i, copies in enumerate(panels):
         for copy in copies:
             copy.wait()
-
-        def multiply(step, carry):
-            here = pl.ds(pl.multiple_of(step * block, block), block)
+        for step, here in enumerate(blocks):
+            if i == 0:
+                row_copies[step].wait()
             both = product(rows[here, :], gate_up[i])
             units_here = jax.nn.silu(both[:, :units]) * both[:, units:]
             hidden_ref[here, i * units : (i + 1) * units] = units_here.astype(jnp.bfloat16)
-            return carry
-
-        lax.fori_loop(0, steps, multiply, 0)
-
-
-def hidden_units(rows, gate, up, gate_other, up_other):
+
+
+def hidden_units(rows, gate, up, gate_other, up_other, steps=2):
     count, features = rows.shape
     units = gate.shape[1]
     return pl.pallas_call(
@@ -138,7 +134,7 @@
         scratch_shapes=[
             pltpu.VMEM((count, features), jnp.bfloat16),
             pltpu.VMEM((2, features, 2 * units), jnp.bfloat16),
-            pltpu.SemaphoreType.DMA((5,)),
+            pltpu.SemaphoreType.DMA((4 + steps,)),
         ],
         compiler_params=pltpu.CompilerParams(vmem_limit_bytes=HIDDEN_VMEM_BYTES),
         cost_estimate=pl.CostEstimate(
@@ -156,7 +152,7 @@
     part_ref[...] = total.astype(part_ref.dtype)
 
 
-def down_part(hidden, down, down_other, steps=4):
+def down_part(hidden, down, down_other, steps=2):
     count = hidden.shape[0]
     units, features = down.shape
     block = features // steps

time: 97.1 us -> 95.9 us (0.988)
  the two profiles are of different devices: /device:TPU:224 before, /device:TPU:96 now
where the time goes in v5:
time: 95.9 us; the launch traced here: 95.5 us
  blocking collectives  71.5 us (75%)
  starting transfers between devices  11.2 us (12%)
  Pallas kernels  10.4 us (11%)
  other arithmetic  2.2 us (2%)
    all_to_all x2, blocking collectives, exchange(): lax.all_to_all(blocks, everywhere, split_axis=0, concat_axis=0, axis_inde...  71.5 us
    pallas_call x1, Pallas kernels, hidden_units(): pl.pallas_call(hidden_kernel, out_shape=jax.ShapeDtypeStruct((count, 2 *...  4.68 us
    ppermute x1, starting transfers between devices, local(): gate_other = lax.ppermute(w_gate[0], everywhere, swap)  3.4 us
    ppermute x1, starting transfers between devices, local(): down_other = lax.ppermute(w_down[0], everywhere, swap)  3.4 us
    ppermute x1, starting transfers between devices, local(): up_other = lax.ppermute(w_up[0], everywhere, swap)  2.45 us
    pallas_call x1, Pallas kernels, front(): pl.pallas_call(front_kernel, out_shape=(jax.ShapeDtypeStruct((tokens, fea...  2.11 us
  transfers between devices with their start and end apart: 4, of which 1 were waited for; matrix products, arithmetic and copies ran while one was open for 2% of the time, Pallas kernels for 7%

profile of v5, /device:TPU:96, one launch (start us, length us, event | category | flops | bytes accessed | tf_op | source)
XLA Modules:
  0.0 95.5 jit_solution(7048189701099453482)
XLA Ops:
  0.0 1.9 %collective-permute-start = (bf16[192,2048]{1,0:T(8,128)(2,1)}, bf16[192,2048]{1,0:T(8,128)(2,1)S(1)}, u32[]{:S(2)}, u32[]{:S(2)}) collective-permute-start(bf16[192,2048]{1,0:T(8,128)(2,1)} %bitcast.26), channel_id=1, source_target_pairs={{0,16},{16,32},{32,48},{48,64},{64,80},{80,96},{96,112},{112,128},... | collective-permute-start | bytes 2359304 | tf_op jit(solution)/shard_map/ppermute | solution.py:16
  1.9 3.4 %collective-permute-start.1 = (bf16[2048,256]{1,0:T(8,128)(2,1)}, bf16[2048,256]{1,0:T(8,128)(2,1)}, u32[]{:S(2)}, u32[]{:S(2)}) collective-permute-start(bf16[2048,256]{1,0:T(8,128)(2,1)} %bitcast.20), channel_id=1, source_target_pairs={{0,1},{1,0},{2,3},{3,2},{4,5},{5,4},{6,7},{7,6},{8,9},{9,8},{10,11... | collective-permute-start | bytes 3145736 | tf_op jit(solution)/shard_map/ppermute | solution.py:231
  5.3 2.4 %collective-permute-start.2 = (bf16[2048,256]{1,0:T(8,128)(2,1)}, bf16[2048,256]{1,0:T(8,128)(2,1)}, u32[]{:S(2)}, u32[]{:S(2)}) collective-permute-start(bf16[2048,256]{1,0:T(8,128)(2,1)} %bitcast.24), channel_id=1, source_target_pairs={{0,1},{1,0},{2,3},{3,2},{4,5},{5,4},{6,7},{7,6},{8,9},{9,8},{10,11... | collective-permute-start | bytes 3145736 | tf_op jit(solution)/shard_map/ppermute | solution.py:232
  7.8 3.4 %collective-permute-start.3 = (bf16[256,2048]{1,0:T(8,128)(2,1)}, bf16[256,2048]{1,0:T(8,128)(2,1)S(1)}, u32[]{:S(2)}, u32[]{:S(2)}) collective-permute-start(bf16[256,2048]{1,0:T(8,128)(2,1)} %bitcast.18), channel_id=1, source_target_pairs={{0,1},{1,0},{2,3},{3,2},{4,5},{5,4},{6,7},{7,6},{8,9},{9,8},{10,11... | collective-permute-start | bytes 3145736 | tf_op jit(solution)/shard_map/ppermute | solution.py:233
  11.2 0.7 convert_bitcast_fusion
  11.9 0.7 convert_bitcast_fusion.1
  12.6 0.7 convert_element_type.38
  13.3 0.1 broadcast_select_fusion.entering_ref
  13.4 0.1 collective-permute-done.arrived_ref
  13.5 2.1 %shard_map.82 = (bf16[192,2048]{1,0:T(8,128)(2,1)S(1)}, f32[192,1]{1,0:T(8,128)S(1)}, s32[192,1]{1,0:T(8,128)S(1)}, bf16[576,2048]{1,0:T(8,128)(2,1)}) custom-call(s32[1]{0:T(128)} %bitcast.2.first_ref, f32[6,2048]{1,0:T(8,128)S(1)} %select_maximum_fusion.small_ref, bf16[192,2048]{1,0:T(8,128)(2,1)S(1)} %collective-permute-done.arrived_ref, ...), custom_call_target="tpu_custom_call" | custom-call | flops 9059696640 | bytes 4718592 | tf_op jit(solution)/shard_map/pallas_call | solution.py:77
  15.6 0.0 copy-start.1
  15.6 39.4 %conditional.1 = (bf16[576,2048]{1,0:T(8,128)(2,1)}) conditional(s32[]{:T(128)} %convert_element_type.41, () %tuple.11, bf16[576,2048]{1,0:T(8,128)(2,1)} %get-tuple-element.14), branch_computations={%region_0.1_spmd, %region_1.2_spmd} | conditional | bytes 4718600 | solution.py:250
  15.6 39.3 %all_to_all.20 = bf16[8,72,2048]{2,1,0:T(8,128)(2,1)} all-to-all(bf16[8,72,2048]{2,1,0:T(8,128)(2,1)} %bitcast.23), channel_id=1, replica_groups={{0,3,4,7,8,11,12,15},{1,2,5,6,9,10,13,14},{16,17,20,21,24,25,28,29},{18..., dimensions={0} | all-to-all | bytes 4718592 | tf_op jit(solution)/shard_map/cond/branch_1_fun/all_to_all | solution.py:242
  55.0 0.0 copy-start
  55.0 0.0 collective-permute-done.1.gate_other_ref
  55.0 0.0 collective-permute-done.2.up_other_ref
  55.0 0.0 copy-done.1
  55.0 4.7 %shard_map.83.hidden_ref = bf16[576,512]{1,0:T(8,128)(2,1)S(1)} custom-call(bf16[576,2048]{1,0:T(8,128)(2,1)} %get-tuple-element.17.rows_ref, bf16[2048,256]{1,0:T(8,128)(2,1)S(1)} %bitcast.21, bf16[2048,256]{1,0:T(8,128)(2,1)} %bitcast.25, bf16[2048,256]{1,0:T(8,128)(2,1)} %collective-permute-done.1.gate_other_ref, ...), custom_call_target="tpu_custom_call" | custom-call | flops 2415919104 | bytes 6553600 | tf_op jit(solution)/shard_map/pallas_call | solution.py:129
  59.7 0.0 collective-permute-done.3.down_other_ref
  59.7 0.0 copy-done
  59.7 1.9 %shard_map.84 = bf16[576,2048]{1,0:T(8,128)(2,1)S(1)} custom-call(bf16[576,512]{1,0:T(8,128)(2,1)S(1)} %shard_map.83.hidden_ref, bf16[256,2048]{1,0:T(8,128)(2,1)S(1)} %bitcast.19, bf16[256,2048]{1,0:T(8,128)(2,1)S(1)} %collective-permute-done.3.down_other_ref), custom_call_target="tpu_custom_call" | custom-call | flops 1207959552 | bytes 5046272 | tf_op jit(solution)/shard_map/pallas_call | solution.py:159
  61.6 32.1 %all_to_all.21 = bf16[8,72,2048]{2,1,0:T(8,128)(2,1)S(1)} all-to-all(bf16[8,72,2048]{2,1,0:T(8,128)(2,1)S(1)} %bitcast.16), channel_id=1, replica_groups={{0,3,4,7,8,11,12,15},{1,2,5,6,9,10,13,14},{16,17,20,21,24,25,28,29},{18..., dimensions={0} | all-to-all | bytes 4718592 | tf_op jit(solution)/shard_map/all_to_all | solution.py:242
  93.8 1.7 %shard_map.85 = bf16[1,192,2048]{2,1,0:T(8,128)(2,1)} custom-call(s32[192,1]{1,0:T(8,128)S(1)} %get-tuple-element.13.place_ref, bf16[576,2048]{1,0:T(8,128)(2,1)S(1)} %bitcast.17, bf16[192,2048]{1,0:T(8,128)(2,1)S(1)} %get-tuple-element.15.arriving_ref, f32[192,1]{1,0:T(8,128)S(1)} %get-tuple-element.16.gate_ref), custom_call_target="tpu_custom_call" | custom-call | flops 452984832 | bytes 3932160 | tf_op jit(solution)/shard_map/pallas_call | solution.py:192
  (1 shorter events, 0.0 us)
Async XLA Ops:
  0.0 13.5 %collective-permute-start = (bf16[192,2048]{1,0:T(8,128)(2,1)}, bf16[192,2048]{1,0:T(8,128)(2,1)S(1)}, u32[]{:S(2)}, u32[]{:S(2)}) collective-permute-start(bf16[192,2048]{1,0:T(8,128)(2,1)} %bitcast.26), channel_id=1, source_target_pairs={{0,16},{16,32},{32,48},{48,64},{64,80},{80,96},{96,112},{112,128},... | collective-permute-start | bytes 2359304 | tf_op jit(solution)/shard_map/ppermute | solution.py:16
  1.9 53.1 %collective-permute-start.1 = (bf16[2048,256]{1,0:T(8,128)(2,1)}, bf16[2048,256]{1,0:T(8,128)(2,1)}, u32[]{:S(2)}, u32[]{:S(2)}) collective-permute-start(bf16[2048,256]{1,0:T(8,128)(2,1)} %bitcast.20), channel_id=1, source_target_pairs={{0,1},{1,0},{2,3},{3,2},{4,5},{5,4},{6,7},{7,6},{8,9},{9,8},{10,11... | collective-permute-start | bytes 3145736 | tf_op jit(solution)/shard_map/ppermute | solution.py:231
  5.3 49.7 %collective-permute-start.2 = (bf16[2048,256]{1,0:T(8,128)(2,1)}, bf16[2048,256]{1,0:T(8,128)(2,1)}, u32[]{:S(2)}, u32[]{:S(2)}) collective-permute-start(bf16[2048,256]{1,0:T(8,128)(2,1)} %bitcast.24), channel_id=1, source_target_pairs={{0,1},{1,0},{2,3},{3,2},{4,5},{5,4},{6,7},{7,6},{8,9},{9,8},{10,11... | collective-permute-start | bytes 3145736 | tf_op jit(solution)/shard_map/ppermute | solution.py:232
  7.8 51.9 %collective-permute-start.3 = (bf16[256,2048]{1,0:T(8,128)(2,1)}, bf16[256,2048]{1,0:T(8,128)(2,1)S(1)}, u32[]{:S(2)}, u32[]{:S(2)}) collective-permute-start(bf16[256,2048]{1,0:T(8,128)(2,1)} %bitcast.18), channel_id=1, source_target_pairs={{0,1},{1,0},{2,3},{3,2},{4,5},{5,4},{6,7},{7,6},{8,9},{9,8},{10,11... | collective-permute-start | bytes 3145736 | tf_op jit(solution)/shard_map/ppermute | solution.py:233
  15.6 39.4 %copy-start.1 = (bf16[1,2048,256]{2,1,0:T(8,128)(2,1)S(1)}, bf16[1,2048,256]{2,1,0:T(8,128)(2,1)}, u32[]{:S(2)}) copy-start(bf16[1,2048,256]{2,1,0:T(8,128)(2,1)} %param.14) | copy-start | bytes 3145732
  55.0 4.7 %copy-start = (bf16[1,256,2048]{2,1,0:T(8,128)(2,1)S(1)}, bf16[1,256,2048]{2,1,0:T(8,128)(2,1)}, u32[]{:S(2)}) copy-start(bf16[1,256,2048]{2,1,0:T(8,128)(2,1)} %param.16) | copy-start | bytes 3145732

commit v6 on v5

--- a/solution.py
+++ b/solution.py
@@ -235,8 +235,9 @@
 
     first = (lax.axis_index("section") == 0).astype(jnp.int32).reshape(1)
 
-    chosen = jnp.pad(expert_ids[0].T.astype(jnp.float32), ((0, 0), (0, features - tokens)))
-    small = jnp.concatenate([router[0].T.astype(jnp.float32), norm_gain.astype(jnp.float32), chosen], axis=0)
+    numbers = jnp.pad(expert_ids[0].T, ((experts + 1, 0), (0, features - tokens)))
+    small = jnp.pad(router[0].T, ((0, 2), (0, 0))) + jnp.pad(norm_gain, ((experts, 1), (0, 0)))
+    small = small.astype(jnp.float32) + numbers.astype(jnp.float32)
 
     def exchange(blocks):
         return lax.all_to_all(

time: 95.9 us -> 95.7 us (level)
  the two profiles are of different devices: /device:TPU:96 before, /device:TPU:102 now
where the time goes in v6:
time: 95.7 us; the launch traced here: 95.3 us
  blocking collectives  71.3 us (75%)
  starting transfers between devices  10.5 us (11%)
  Pallas kernels  10.4 us (11%)
  waiting for transfers between devices  2.13 us (2%)
    all_to_all x2, blocking collectives, exchange(): lax.all_to_all(blocks, everywhere, split_axis=0, concat_axis=0, axis_inde...  71.3 us
    pallas_call x1, Pallas kernels, hidden_units(): pl.pallas_call(hidden_kernel, out_shape=jax.ShapeDtypeStruct((count, 2 *...  4.68 us
    ppermute x1, starting transfers between devices, local(): up_other = lax.ppermute(w_up[0], everywhere, swap)  3.11 us
    ppermute x1, starting transfers between devices, local(): gate_other = lax.ppermute(w_gate[0], everywhere, swap)  2.74 us
    ppermute x1, starting transfers between devices, local(): down_other = lax.ppermute(w_down[0], everywhere, swap)  2.74 us
    ppermute x1, waiting for transfers between devices, passed_along(): return lax.ppermute(block, axis, route)  2.12 us
    pallas_call x1, Pallas kernels, front(): pl.pallas_call(front_kernel, out_shape=(jax.ShapeDtypeStruct((tokens, fea...  2.1 us
  transfers between devices with their start and end apart: 4, of which 1 were waited for; matrix products, arithmetic and copies ran while one was open for 1% of the time, Pallas kernels for 7%

profile of v6, /device:TPU:102, one launch (start us, length us, event | category | flops | bytes accessed | tf_op | source)
XLA Modules:
  0.0 95.3 jit_solution(15563259753401215255)
XLA Ops:
  0.0 1.9 %collective-permute-start = (bf16[192,2048]{1,0:T(8,128)(2,1)}, bf16[192,2048]{1,0:T(8,128)(2,1)S(1)}, u32[]{:S(2)}, u32[]{:S(2)}) collective-permute-start(bf16[192,2048]{1,0:T(8,128)(2,1)} %bitcast.25), channel_id=1, source_target_pairs={{0,16},{16,32},{32,48},{48,64},{64,80},{80,96},{96,112},{112,128},... | collective-permute-start | bytes 2359304 | tf_op jit(solution)/shard_map/ppermute | solution.py:16
  1.9 2.7 %collective-permute-start.1 = (bf16[2048,256]{1,0:T(8,128)(2,1)}, bf16[2048,256]{1,0:T(8,128)(2,1)}, u32[]{:S(2)}, u32[]{:S(2)}) collective-permute-start(bf16[2048,256]{1,0:T(8,128)(2,1)} %bitcast.17), channel_id=1, source_target_pairs={{0,1},{1,0},{2,3},{3,2},{4,5},{5,4},{6,7},{7,6},{8,9},{9,8},{10,11... | collective-permute-start | bytes 3145736 | tf_op jit(solution)/shard_map/ppermute | solution.py:231
  4.7 3.1 %collective-permute-start.2 = (bf16[2048,256]{1,0:T(8,128)(2,1)}, bf16[2048,256]{1,0:T(8,128)(2,1)}, u32[]{:S(2)}, u32[]{:S(2)}) collective-permute-start(bf16[2048,256]{1,0:T(8,128)(2,1)} %bitcast.23), channel_id=1, source_target_pairs={{0,1},{1,0},{2,3},{3,2},{4,5},{5,4},{6,7},{7,6},{8,9},{9,8},{10,11... | collective-permute-start | bytes 3145736 | tf_op jit(solution)/shard_map/ppermute | solution.py:232
  7.8 2.7 %collective-permute-start.3 = (bf16[256,2048]{1,0:T(8,128)(2,1)}, bf16[256,2048]{1,0:T(8,128)(2,1)S(1)}, u32[]{:S(2)}, u32[]{:S(2)}) collective-permute-start(bf16[256,2048]{1,0:T(8,128)(2,1)} %bitcast.15), channel_id=1, source_target_pairs={{0,1},{1,0},{2,3},{3,2},{4,5},{5,4},{6,7},{7,6},{8,9},{9,8},{10,11... | collective-permute-start | bytes 3145736 | tf_op jit(solution)/shard_map/ppermute | solution.py:233
  10.5 0.1 broadcast_select_fusion.entering_ref
  10.6 0.8 convert_add_fusion.small_ref
  11.4 2.1 %collective-permute-done.arrived_ref = bf16[192,2048]{1,0:T(8,128)(2,1)S(1)} collective-permute-done((bf16[192,2048]{1,0:T(8,128)(2,1)}, bf16[192,2048]{1,0:T(8,128)(2,1)S(1)}, u32[]{:S(2)}, u32[]{:S(2)}) %collective-permute-start) | collective-permute-done | bytes 786464 | tf_op jit(solution)/shard_map/ppermute | solution.py:16
  13.5 2.1 %shard_map.82 = (bf16[192,2048]{1,0:T(8,128)(2,1)S(1)}, f32[192,1]{1,0:T(8,128)S(1)}, s32[192,1]{1,0:T(8,128)S(1)}, bf16[576,2048]{1,0:T(8,128)(2,1)}) custom-call(s32[1]{0:T(128)} %bitcast.2.first_ref, f32[6,2048]{1,0:T(8,128)S(1)} %convert_add_fusion.small_ref, bf16[192,2048]{1,0:T(8,128)(2,1)S(1)} %collective-permute-done.arrived_ref, ...), custom_call_target="tpu_custom_call" | custom-call | flops 9059696640 | bytes 4718592 | tf_op jit(solution)/shard_map/pallas_call | solution.py:77
  15.6 0.0 copy-start.1
  15.6 36.8 %conditional.1 = (bf16[576,2048]{1,0:T(8,128)(2,1)}) conditional(s32[]{:T(128)} %convert_element_type.19, () %tuple.11, bf16[576,2048]{1,0:T(8,128)(2,1)} %get-tuple-element.14), branch_computations={%region_0.1_spmd, %region_1.2_spmd} | conditional | bytes 4718600 | solution.py:251
  15.6 36.7 %all_to_all.20 = bf16[8,72,2048]{2,1,0:T(8,128)(2,1)} all-to-all(bf16[8,72,2048]{2,1,0:T(8,128)(2,1)} %bitcast.20), channel_id=1, replica_groups={{0,3,4,7,8,11,12,15},{1,2,5,6,9,10,13,14},{16,17,20,21,24,25,28,29},{18..., dimensions={0} | all-to-all | bytes 4718592 | tf_op jit(solution)/shard_map/cond/branch_1_fun/all_to_all | solution.py:243
  52.4 0.0 copy-start
  52.4 0.0 collective-permute-done.1.gate_other_ref
  52.4 0.0 collective-permute-done.2.up_other_ref
  52.4 0.0 copy-done.1
  52.4 4.7 %shard_map.83.hidden_ref = bf16[576,512]{1,0:T(8,128)(2,1)S(1)} custom-call(bf16[576,2048]{1,0:T(8,128)(2,1)} %get-tuple-element.17.rows_ref, bf16[2048,256]{1,0:T(8,128)(2,1)S(1)} %bitcast.18, bf16[2048,256]{1,0:T(8,128)(2,1)} %bitcast.24, bf16[2048,256]{1,0:T(8,128)(2,1)} %collective-permute-done.1.gate_other_ref, ...), custom_call_target="tpu_custom_call" | custom-call | flops 2415919104 | bytes 6553600 | tf_op jit(solution)/shard_map/pallas_call | solution.py:129
  57.1 0.0 collective-permute-done.3.down_other_ref
  57.1 0.0 copy-done
  57.1 1.9 %shard_map.84 = bf16[576,2048]{1,0:T(8,128)(2,1)S(1)} custom-call(bf16[576,512]{1,0:T(8,128)(2,1)S(1)} %shard_map.83.hidden_ref, bf16[256,2048]{1,0:T(8,128)(2,1)S(1)} %bitcast.16, bf16[256,2048]{1,0:T(8,128)(2,1)S(1)} %collective-permute-done.3.down_other_ref), custom_call_target="tpu_custom_call" | custom-call | flops 1207959552 | bytes 5046272 | tf_op jit(solution)/shard_map/pallas_call | solution.py:159
  59.0 34.6 %all_to_all.21 = bf16[8,72,2048]{2,1,0:T(8,128)(2,1)S(1)} all-to-all(bf16[8,72,2048]{2,1,0:T(8,128)(2,1)S(1)} %bitcast.13), channel_id=1, replica_groups={{0,3,4,7,8,11,12,15},{1,2,5,6,9,10,13,14},{16,17,20,21,24,25,28,29},{18..., dimensions={0} | all-to-all | bytes 4718592 | tf_op jit(solution)/shard_map/all_to_all | solution.py:243
  93.6 1.7 %shard_map.85 = bf16[1,192,2048]{2,1,0:T(8,128)(2,1)} custom-call(s32[192,1]{1,0:T(8,128)S(1)} %get-tuple-element.13.place_ref, bf16[576,2048]{1,0:T(8,128)(2,1)S(1)} %bitcast.14, bf16[192,2048]{1,0:T(8,128)(2,1)S(1)} %get-tuple-element.15.arriving_ref, f32[192,1]{1,0:T(8,128)S(1)} %get-tuple-element.16.gate_ref), custom_call_target="tpu_custom_call" | custom-call | flops 452984832 | bytes 3932160 | tf_op jit(solution)/shard_map/pallas_call | solution.py:192
Async XLA Ops:
  0.0 13.5 %collective-permute-start = (bf16[192,2048]{1,0:T(8,128)(2,1)}, bf16[192,2048]{1,0:T(8,128)(2,1)S(1)}, u32[]{:S(2)}, u32[]{:S(2)}) collective-permute-start(bf16[192,2048]{1,0:T(8,128)(2,1)} %bitcast.25), channel_id=1, source_target_pairs={{0,16},{16,32},{32,48},{48,64},{64,80},{80,96},{96,112},{112,128},... | collective-permute-start | bytes 2359304 | tf_op jit(solution)/shard_map/ppermute | solution.py:16
  1.9 50.5 %collective-permute-start.1 = (bf16[2048,256]{1,0:T(8,128)(2,1)}, bf16[2048,256]{1,0:T(8,128)(2,1)}, u32[]{:S(2)}, u32[]{:S(2)}) collective-permute-start(bf16[2048,256]{1,0:T(8,128)(2,1)} %bitcast.17), channel_id=1, source_target_pairs={{0,1},{1,0},{2,3},{3,2},{4,5},{5,4},{6,7},{7,6},{8,9},{9,8},{10,11... | collective-permute-start | bytes 3145736 | tf_op jit(solution)/shard_map/ppermute | solution.py:231
  4.7 47.7 %collective-permute-start.2 = (bf16[2048,256]{1,0:T(8,128)(2,1)}, bf16[2048,256]{1,0:T(8,128)(2,1)}, u32[]{:S(2)}, u32[]{:S(2)}) collective-permute-start(bf16[2048,256]{1,0:T(8,128)(2,1)} %bitcast.23), channel_id=1, source_target_pairs={{0,1},{1,0},{2,3},{3,2},{4,5},{5,4},{6,7},{7,6},{8,9},{9,8},{10,11... | collective-permute-start | bytes 3145736 | tf_op jit(solution)/shard_map/ppermute | solution.py:232
  7.8 49.3 %collective-permute-start.3 = (bf16[256,2048]{1,0:T(8,128)(2,1)}, bf16[256,2048]{1,0:T(8,128)(2,1)S(1)}, u32[]{:S(2)}, u32[]{:S(2)}) collective-permute-start(bf16[256,2048]{1,0:T(8,128)(2,1)} %bitcast.15), channel_id=1, source_target_pairs={{0,1},{1,0},{2,3},{3,2},{4,5},{5,4},{6,7},{7,6},{8,9},{9,8},{10,11... | collective-permute-start | bytes 3145736 | tf_op jit(solution)/shard_map/ppermute | solution.py:233
  15.6 36.8 %copy-start.1 = (bf16[1,2048,256]{2,1,0:T(8,128)(2,1)S(1)}, bf16[1,2048,256]{2,1,0:T(8,128)(2,1)}, u32[]{:S(2)}) copy-start(bf16[1,2048,256]{2,1,0:T(8,128)(2,1)} %param.14) | copy-start | bytes 3145732
  52.4 4.7 %copy-start = (bf16[1,256,2048]{2,1,0:T(8,128)(2,1)S(1)}, bf16[1,256,2048]{2,1,0:T(8,128)(2,1)}, u32[]{:S(2)}) copy-start(bf16[1,256,2048]{2,1,0:T(8,128)(2,1)} %param.16) | copy-start | bytes 3145732

commit v7 on v6

--- a/solution.py
+++ b/solution.py
@@ -95,10 +95,10 @@
     )(first, small, arrived, entering)
 
 
-def hidden_kernel(rows_ref, gate_ref, up_ref, gate_other_ref, up_other_ref, hidden_ref, rows, gate_up, in_sems):
+def hidden_kernel(rows_ref, gate_ref, up_ref, gate_other_ref, up_other_ref, down_ref, hidden_ref, own_ref, rows, gate_up, down, in_sems):
     count, features = rows.shape
     units = gate_ref.shape[1]
-    steps = in_sems.shape[0] - 4
+    steps = in_sems.shape[0] - 5
     block = count // steps
 
     def fetch(source, target, index):
@@ -112,6 +112,7 @@
     panels = [(fetch(gate_ref, gate_up.at[0, :, first], 0), fetch(up_ref, gate_up.at[0, :, second], 1))]
     row_copies += [fetch(rows_ref.at[blocks[i]], rows.at[blocks[i]], 4 + i) for i in range(1, steps)]
     panels += [(fetch(gate_other_ref, gate_up.at[1, :, first], 2), fetch(up_other_ref, gate_up.at[1, :, second], 3))]
+    down_copy = fetch(down_ref, down, 4 + steps)
     for i, copies in enumerate(panels):
         for copy in copies:
             copy.wait()
@@ -120,21 +121,31 @@
                 row_copies[step].wait()
             both = product(rows[here, :], gate_up[i])
             units_here = jax.nn.silu(both[:, :units]) * both[:, units:]
-            hidden_ref[here, i * units : (i + 1) * units] = units_here.astype(jnp.bfloat16)
-
-
-def hidden_units(rows, gate, up, gate_other, up_other, steps=2):
+            hidden = units_here.astype(jnp.bfloat16)
+            if i == 0:
+                if step == 0:
+                    down_copy.wait()
+                own_ref[here, :] = product(hidden, down[...])
+            else:
+                hidden_ref[here, :] = hidden
+
+
+def hidden_units(rows, gate, up, gate_other, up_other, down, steps=2):
     count, features = rows.shape
     units = gate.shape[1]
     return pl.pallas_call(
         hidden_kernel,
-        out_shape=jax.ShapeDtypeStruct((count, 2 * units), jnp.bfloat16),
-        in_specs=[anywhere()] * 5,
-        out_specs=pl.BlockSpec(memory_space=pltpu.VMEM),
+        out_shape=(
+            jax.ShapeDtypeStruct((count, units), jnp.bfloat16),
+            jax.ShapeDtypeStruct((count, features), jnp.float32),
+        ),
+        in_specs=[anywhere()] * 6,
+        out_specs=(pl.BlockSpec(memory_space=pltpu.VMEM), pl.BlockSpec(memory_space=pltpu.VMEM)),
         scratch_shapes=[
             pltpu.VMEM((count, features), jnp.bfloat16),
             pltpu.VMEM((2, features, 2 * units), jnp.bfloat16),
-            pltpu.SemaphoreType.DMA((4 + steps,)),
+            pltpu.VMEM((units, features), jnp.bfloat16),
+            pltpu.SemaphoreType.DMA((5 + steps,)),
         ],
         compiler_params=pltpu.CompilerParams(vmem_limit_bytes=HIDDEN_VMEM_BYTES),
         cost_estimate=pl.CostEstimate(
@@ -142,37 +153,35 @@
             bytes_accessed=2 * (count * features + 4 * features * units),
             transcendentals=2 * count * units,
         ),
-    )(rows, gate, up, gate_other, up_other)
-
-
-def down_kernel(hidden_ref, down_ref, down_other_ref, part_ref):
-    units = down_ref.shape[0]
-    total = product(hidden_ref[:, :units], down_ref[...])
-    total += product(hidden_ref[:, units:], down_other_ref[...])
+    )(rows, gate, up, gate_other, up_other, down)
+
+
+def down_kernel(own_ref, hidden_ref, down_ref, part_ref):
+    total = own_ref[...] + product(hidden_ref[...], down_ref[...])
     part_ref[...] = total.astype(part_ref.dtype)
 
 
-def down_part(hidden, down, down_other, steps=2):
-    count = hidden.shape[0]
-    units, features = down.shape
+def down_part(own, hidden, down_other, steps=2):
+    count, units = hidden.shape
+    features = down_other.shape[1]
     block = features // steps
     return pl.pallas_call(
         down_kernel,
         grid=(steps,),
         out_shape=jax.ShapeDtypeStruct((count, features), jnp.bfloat16),
         in_specs=[
-            pl.BlockSpec((count, 2 * units), lambda i: (0, 0)),
-            pl.BlockSpec((units, block), lambda i: (0, i)),
+            pl.BlockSpec((count, block), lambda i: (0, i)),
+            pl.BlockSpec((count, units), lambda i: (0, 0)),
             pl.BlockSpec((units, block), lambda i: (0, i)),
         ],
         out_specs=pl.BlockSpec((count, block), lambda i: (0, i)),
         compiler_params=pltpu.CompilerParams(vmem_limit_bytes=VMEM_BYTES),
         cost_estimate=pl.CostEstimate(
-            flops=4 * count * features * units,
-            bytes_accessed=2 * (count * (features + 2 * units) + 2 * features * units),
+            flops=2 * count * features * units,
+            bytes_accessed=6 * count * features + 2 * units * (count + features),
             transcendentals=0,
         ),
-    )(hidden, down, down_other)
+    )(own, hidden, down_other)
 
 
 def combine_kernel(place_ref, returned_ref, arriving_ref, gate_ref, mixed_ref):
@@ -249,8 +258,8 @@
     )
     here = lax.axis_index("section") < sections
     rows = lax.cond(here, exchange, jnp.zeros_like, sent)
-    hidden = hidden_units(rows, w_gate[0], w_up[0], gate_other, up_other)
-    part = down_part(hidden, w_down[0], down_other)
+    hidden, own = hidden_units(rows, w_gate[0], w_up[0], gate_other, up_other, w_down[0])
+    part = down_part(own, hidden, down_other)
     return combine(place, exchange(part), arriving, gate_value)
 
 

time: 95.7 us -> 97.8 us (1.022)
  the two profiles are of different devices: /device:TPU:102 before, /device:TPU:224 now
where the time goes in v7:
time: 97.8 us; the launch traced here: 97.4 us
  blocking collectives  70.3 us (72%)
  Pallas kernels  13.5 us (14%)
  starting transfers between devices  11.2 us (11%)
  waiting for transfers between devices  1.47 us (2%)
    all_to_all x2, blocking collectives, exchange(): lax.all_to_all(blocks, everywhere, split_axis=0, concat_axis=0, axis_inde...  70.3 us
    pallas_call x1, Pallas kernels, hidden_units(): pl.pallas_call(hidden_kernel, out_shape=(jax.ShapeDtypeStruct((count, uni...  6.76 us
    ppermute x1, starting transfers between devices, local(): gate_other = lax.ppermute(w_gate[0], everywhere, swap)  3.4 us
    ppermute x1, starting transfers between devices, local(): down_other = lax.ppermute(w_down[0], everywhere, swap)  3.4 us
    pallas_call x1, Pallas kernels, down_part(): pl.pallas_call(down_kernel, grid=(steps,), out_shape=jax.ShapeDtypeStruct...  2.97 us
    ppermute x1, starting transfers between devices, local(): up_other = lax.ppermute(w_up[0], everywhere, swap)  2.45 us
    pallas_call x1, Pallas kernels, front(): pl.pallas_call(front_kernel, out_shape=(jax.ShapeDtypeStruct((tokens, fea...  2.1 us
  transfers between devices with their start and end apart: 4, of which 1 were waited for; matrix products, arithmetic and copies ran while one was open for 1% of the time, Pallas kernels for 9%

profile of v7, /device:TPU:224, one launch (start us, length us, event | category | flops | bytes accessed | tf_op | source)
XLA Modules:
  0.0 97.4 jit_solution(17670181873062252615)
XLA Ops:
  0.0 1.9 %collective-permute-start = (bf16[192,2048]{1,0:T(8,128)(2,1)}, bf16[192,2048]{1,0:T(8,128)(2,1)S(1)}, u32[]{:S(2)}, u32[]{:S(2)}) collective-permute-start(bf16[192,2048]{1,0:T(8,128)(2,1)} %bitcast.25), channel_id=1, source_target_pairs={{0,16},{16,32},{32,48},{48,64},{64,80},{80,96},{96,112},{112,128},... | collective-permute-start | bytes 2359304 | tf_op jit(solution)/shard_map/ppermute | solution.py:16
  1.9 3.4 %collective-permute-start.1 = (bf16[2048,256]{1,0:T(8,128)(2,1)}, bf16[2048,256]{1,0:T(8,128)(2,1)}, u32[]{:S(2)}, u32[]{:S(2)}) collective-permute-start(bf16[2048,256]{1,0:T(8,128)(2,1)} %bitcast.15), channel_id=1, source_target_pairs={{0,1},{1,0},{2,3},{3,2},{4,5},{5,4},{6,7},{7,6},{8,9},{9,8},{10,11... | collective-permute-start | bytes 3145736 | tf_op jit(solution)/shard_map/ppermute | solution.py:240
  5.3 2.4 %collective-permute-start.2 = (bf16[2048,256]{1,0:T(8,128)(2,1)}, bf16[2048,256]{1,0:T(8,128)(2,1)}, u32[]{:S(2)}, u32[]{:S(2)}) collective-permute-start(bf16[2048,256]{1,0:T(8,128)(2,1)} %bitcast.21), channel_id=1, source_target_pairs={{0,1},{1,0},{2,3},{3,2},{4,5},{5,4},{6,7},{7,6},{8,9},{9,8},{10,11... | collective-permute-start | bytes 3145736 | tf_op jit(solution)/shard_map/ppermute | solution.py:241
  7.8 3.4 %collective-permute-start.3 = (bf16[256,2048]{1,0:T(8,128)(2,1)}, bf16[256,2048]{1,0:T(8,128)(2,1)S(1)}, u32[]{:S(2)}, u32[]{:S(2)}) collective-permute-start(bf16[256,2048]{1,0:T(8,128)(2,1)} %bitcast.23), channel_id=1, source_target_pairs={{0,1},{1,0},{2,3},{3,2},{4,5},{5,4},{6,7},{7,6},{8,9},{9,8},{10,11... | collective-permute-start | bytes 3145736 | tf_op jit(solution)/shard_map/ppermute | solution.py:242
  11.2 0.1 broadcast_select_fusion.entering_ref
  11.3 0.8 convert_add_fusion.small_ref
  12.0 1.5 %collective-permute-done.arrived_ref = bf16[192,2048]{1,0:T(8,128)(2,1)S(1)} collective-permute-done((bf16[192,2048]{1,0:T(8,128)(2,1)}, bf16[192,2048]{1,0:T(8,128)(2,1)S(1)}, u32[]{:S(2)}, u32[]{:S(2)}) %collective-permute-start) | collective-permute-done | bytes 786464 | tf_op jit(solution)/shard_map/ppermute | solution.py:16
  13.5 2.1 %shard_map.82 = (bf16[192,2048]{1,0:T(8,128)(2,1)S(1)}, f32[192,1]{1,0:T(8,128)S(1)}, s32[192,1]{1,0:T(8,128)S(1)}, bf16[576,2048]{1,0:T(8,128)(2,1)}) custom-call(s32[1]{0:T(128)} %bitcast.2.first_ref, f32[6,2048]{1,0:T(8,128)S(1)} %convert_add_fusion.small_ref, bf16[192,2048]{1,0:T(8,128)(2,1)S(1)} %collective-permute-done.arrived_ref, ...), custom_call_target="tpu_custom_call" | custom-call | flops 9059696640 | bytes 4718592 | tf_op jit(solution)/shard_map/pallas_call | solution.py:77
  15.6 0.0 copy-start
  15.6 39.3 %conditional.1 = (bf16[576,2048]{1,0:T(8,128)(2,1)}) conditional(s32[]{:T(128)} %convert_element_type.19, () %tuple.11, bf16[576,2048]{1,0:T(8,128)(2,1)} %get-tuple-element.16), branch_computations={%region_0.1_spmd, %region_1.2_spmd} | conditional | bytes 4718600 | solution.py:260
  15.6 39.3 %all_to_all.20 = bf16[8,72,2048]{2,1,0:T(8,128)(2,1)} all-to-all(bf16[8,72,2048]{2,1,0:T(8,128)(2,1)} %bitcast.18), channel_id=1, replica_groups={{0,3,4,7,8,11,12,15},{1,2,5,6,9,10,13,14},{16,17,20,21,24,25,28,29},{18..., dimensions={0} | all-to-all | bytes 4718592 | tf_op jit(solution)/shard_map/cond/branch_1_fun/all_to_all | solution.py:252
  55.0 0.0 collective-permute-done.1.gate_other_ref
  55.0 0.0 collective-permute-done.2.up_other_ref
  55.0 0.0 copy-done
  55.0 6.8 %shard_map.83 = (bf16[576,256]{1,0:T(8,128)(2,1)S(1)}, f32[576,2048]{1,0:T(8,128)}) custom-call(bf16[576,2048]{1,0:T(8,128)(2,1)} %get-tuple-element.21.rows_ref, bf16[2048,256]{1,0:T(8,128)(2,1)S(1)} %bitcast.16, bf16[2048,256]{1,0:T(8,128)(2,1)} %bitcast.22, bf16[2048,256]{1,0:T(8,128)(2,1)} %collective-permute-done.1.gate_other_ref, ...), custom_call_target="tpu_custom_call" | custom-call | flops 2415919104 | bytes 6553600 | tf_op jit(solution)/shard_map/pallas_call | solution.py:136
  61.8 0.0 collective-permute-done.3.down_ref
  61.8 3.0 %shard_map.84 = bf16[576,2048]{1,0:T(8,128)(2,1)S(1)} custom-call(f32[576,2048]{1,0:T(8,128)} %get-tuple-element.17.own_ref, bf16[576,256]{1,0:T(8,128)(2,1)S(1)} %get-tuple-element.18.hidden_ref, bf16[256,2048]{1,0:T(8,128)(2,1)S(1)} %collective-permute-done.3.down_ref), custom_call_target="tpu_custom_call" | custom-call | flops 603979776 | bytes 8421376 | tf_op jit(solution)/shard_map/pallas_call | solution.py:168
  64.7 31.0 %all_to_all.21 = bf16[8,72,2048]{2,1,0:T(8,128)(2,1)S(1)} all-to-all(bf16[8,72,2048]{2,1,0:T(8,128)(2,1)S(1)} %bitcast.14), channel_id=1, replica_groups={{0,3,4,7,8,11,12,15},{1,2,5,6,9,10,13,14},{16,17,20,21,24,25,28,29},{18..., dimensions={0} | all-to-all | bytes 4718592 | tf_op jit(solution)/shard_map/all_to_all | solution.py:252
  95.7 1.7 %shard_map.85 = bf16[1,192,2048]{2,1,0:T(8,128)(2,1)} custom-call(s32[192,1]{1,0:T(8,128)S(1)} %get-tuple-element.15.place_ref, bf16[576,2048]{1,0:T(8,128)(2,1)S(1)} %bitcast.13, bf16[192,2048]{1,0:T(8,128)(2,1)S(1)} %get-tuple-element.19.arriving_ref, f32[192,1]{1,0:T(8,128)S(1)} %get-tuple-element.20.gate_ref), custom_call_target="tpu_custom_call" | custom-call | flops 452984832 | bytes 3932160 | tf_op jit(solution)/shard_map/pallas_call | solution.py:201
Async XLA Ops:
  0.0 13.5 %collective-permute-start = (bf16[192,2048]{1,0:T(8,128)(2,1)}, bf16[192,2048]{1,0:T(8,128)(2,1)S(1)}, u32[]{:S(2)}, u32[]{:S(2)}) collective-permute-start(bf16[192,2048]{1,0:T(8,128)(2,1)} %bitcast.25), channel_id=1, source_target_pairs={{0,16},{16,32},{32,48},{48,64},{64,80},{80,96},{96,112},{112,128},... | collective-permute-start | bytes 2359304 | tf_op jit(solution)/shard_map/ppermute | solution.py:16
  1.9 53.1 %collective-permute-start.1 = (bf16[2048,256]{1,0:T(8,128)(2,1)}, bf16[2048,256]{1,0:T(8,128)(2,1)}, u32[]{:S(2)}, u32[]{:S(2)}) collective-permute-start(bf16[2048,256]{1,0:T(8,128)(2,1)} %bitcast.15), channel_id=1, source_target_pairs={{0,1},{1,0},{2,3},{3,2},{4,5},{5,4},{6,7},{7,6},{8,9},{9,8},{10,11... | collective-permute-start | bytes 3145736 | tf_op jit(solution)/shard_map/ppermute | solution.py:240
  5.3 49.7 %collective-permute-start.2 = (bf16[2048,256]{1,0:T(8,128)(2,1)}, bf16[2048,256]{1,0:T(8,128)(2,1)}, u32[]{:S(2)}, u32[]{:S(2)}) collective-permute-start(bf16[2048,256]{1,0:T(8,128)(2,1)} %bitcast.21), channel_id=1, source_target_pairs={{0,1},{1,0},{2,3},{3,2},{4,5},{5,4},{6,7},{7,6},{8,9},{9,8},{10,11... | collective-permute-start | bytes 3145736 | tf_op jit(solution)/shard_map/ppermute | solution.py:241
  7.8 54.0 %collective-permute-start.3 = (bf16[256,2048]{1,0:T(8,128)(2,1)}, bf16[256,2048]{1,0:T(8,128)(2,1)S(1)}, u32[]{:S(2)}, u32[]{:S(2)}) collective-permute-start(bf16[256,2048]{1,0:T(8,128)(2,1)} %bitcast.23), channel_id=1, source_target_pairs={{0,1},{1,0},{2,3},{3,2},{4,5},{5,4},{6,7},{7,6},{8,9},{9,8},{10,11... | collective-permute-start | bytes 3145736 | tf_op jit(solution)/shard_map/ppermute | solution.py:242
  15.6 39.4 %copy-start = (bf16[1,2048,256]{2,1,0:T(8,128)(2,1)S(1)}, bf16[1,2048,256]{2,1,0:T(8,128)(2,1)}, u32[]{:S(2)}) copy-start(bf16[1,2048,256]{2,1,0:T(8,128)(2,1)} %param.14) | copy-start | bytes 3145732
